TPU v7x, 512 devices: a whole 4x8x8 slice. The times are simulated.
512 devices in a mesh: depth: 16 (over z, core), tile: 32 (over x, y).
Axes of the slice: x: 4, y: 8, z: 8, core: 2. Of those that a mesh axis runs over, the one named last changes fastest.
Arguments:
- bricks: bfloat16 [16, 512, 32, 1024], P('depth', 'tile'), may hold values from -8 to 8
- levels: int32 [16, 512], P('depth', 'tile'), may hold values from 0 to 2
- counts: int32 [16, 512, 1024], P('depth', 'tile'), may hold values from 1 to 32
- gains: float32 [16, 512], P('depth', 'tile'), may hold values from 0.002 to 0.03
- ownership: int32 [16, 32, 16], P('depth'), may hold values from 0 to 31, as said below
- tf_slope: float32 [3], replicated, may hold values from 0.5 to 3
Outputs:
- rgba: float32 [4, 16, 32768], P(None, 'depth', 'tile')
- work_share: float32 [16, 32], P('depth', 'tile')
Inputs may be any that keep to these rules, and one draw needn't show every extreme that they name: `ownership`: slot j of tile t in depth slab d belongs to tile (t + s) mod 32, where the shift s depends on d and j only; two slots share a shift only when j - j' is a multiple of 32. So every device renders exactly 16 bricks and takes exactly 1 bricks from each device that sends it any.
All inputs are finite; a program needn't handle non-finite values.
Results may differ from a plain program's by a relative error of at most 0.0034.
Values may be sent and summed in bfloat16 or wider, within the bound.
A program may use at most 64 MiB of HBM per device.

v0:
```python
import jax
import jax.numpy as jnp
from jax import lax
from jax.sharding import PartitionSpec as P


def entering(part, axis, combine, identity):
    place = lax.axis_index(axis)
    gathered = lax.all_gather(part, axis)
    state = jnp.zeros_like(part) + jnp.asarray(identity, part.dtype)

    def one(hop, state):
        return combine(state, lax.dynamic_index_in_dim(gathered, hop, 0, False))

    return lax.fori_loop(0, place, one, state)


def tent_tables(brick_side):
    cell_index = jnp.arange(brick_side, dtype=jnp.float32)
    tables = []
    for level_index in range(3):
        coarse_cells = brick_side * 2**level_index // 4
        coarse_at = jnp.clip(
            (cell_index + 0.5) * (coarse_cells / brick_side) - 0.5, 0.0, coarse_cells - 1.0
        )
        tables.append(jnp.maximum(0.0, 1.0 - jnp.abs(coarse_at[:, None] - cell_index[None, :])))
    return jnp.stack(tables)


def level_worth(level_grid):
    return jnp.where(level_grid == 2, 1.0, jnp.where(level_grid == 1, 0.25, 0.0625)).astype(
        jnp.float32
    )


def level_from_worth(worth_grid):
    return jnp.where(
        worth_grid > 0.5, 2, jnp.where(worth_grid > 0.1, 1, jnp.where(worth_grid > 0.01, 0, -1))
    ).astype(jnp.int32)


def render(brick_data, grade_of, live_count, gain_of, tf_slope, tent_rows, plane_maps, earlier_map):
    brick_count, brick_side, ray_count = brick_data.shape
    highest = lax.Precision.HIGHEST

    def shade(density, block_live, block_gain):
        softened = jax.nn.softplus(density)
        depth_index = jnp.arange(brick_side, dtype=jnp.int32)
        live_mask = depth_index[:, None] < block_live[None, :]
        optical = block_gain * jnp.where(live_mask, softened, 0.0)
        optical_before = jnp.einsum("zs,sq->zq", earlier_map, optical, precision=highest)
        emission = jnp.exp(-optical_before) * (1.0 - jnp.exp(-optical))
        channels = [
            jnp.sum(emission * jax.nn.sigmoid(tf_slope[k] * density), axis=0) for k in range(3)
        ]
        slab_pass = jnp.exp(-(optical_before[-1] + optical[-1]))
        return jnp.stack(channels + [slab_pass], axis=0)

    def level_branch(level_index):
        used = brick_side * 2**level_index // 4

        def branch(block_data, block_live, block_gain):
            cube = block_data.reshape(brick_side, brick_side, brick_side)[:used, :used, :used]
            cube = cube.reshape(used, used * used)
            product = jnp.dot(cube, plane_maps[level_index], preferred_element_type=jnp.float32)
            density = jnp.einsum(
                "za,aq->zq", tent_rows[level_index][:, :used], product, precision=highest
            )
            return shade(density, block_live, block_gain)

        return branch

    def empty_branch(block_data, block_live, block_gain):
        return jnp.zeros((4, ray_count), jnp.float32)

    branches = [level_branch(0), level_branch(1), level_branch(2), empty_branch]

    def one_brick(packed):
        block_data, block_grade, block_live, block_gain = packed
        which = jnp.where(block_grade < 0, 3, block_grade)
        return lax.switch(which, branches, block_data, block_live, block_gain)

    return lax.map(one_brick, (brick_data, grade_of, live_count, gain_of))


def local(bricks, levels, counts, gains, ownership, tf_slope):
    held_bricks = bricks.shape[1]
    brick_side = bricks.shape[2]
    ray_count = bricks.shape[3]
    tent_rows = tent_tables(brick_side)
    plane_maps = []
    for level_index in range(3):
        used = brick_side * 2**level_index // 4
        narrow = tent_rows[level_index][:, :used].T
        plane_maps.append(jnp.kron(narrow, narrow).astype(jnp.bfloat16))
    cell_ids = jnp.arange(brick_side, dtype=jnp.int32)
    earlier_map = (cell_ids[None, :] < cell_ids[:, None]).astype(jnp.float32)
    tile_count = lax.axis_size("tile")
    depth_count = lax.axis_size("depth")
    tile_here = lax.axis_index("tile")
    brick_worth = level_worth(levels[0])
    owner_row = ownership[0]
    owner_of = lax.dynamic_index_in_dim(owner_row, tile_here, 0, keepdims=False)
    slot_ids = jnp.arange(held_bricks, dtype=jnp.int32)
    same_owner = owner_of[:, None] == owner_of[None, :]
    earlier_slot = slot_ids[None, :] < slot_ids[:, None]
    slot_of = jnp.sum(jnp.logical_and(same_owner, earlier_slot), axis=1)
    room_each = max(1, held_bricks // tile_count)
    send_bricks = (
        jnp.zeros((tile_count, room_each, brick_side, ray_count), jnp.bfloat16)
        .at[owner_of, slot_of]
        .set(bricks[0])
    )
    send_counts = (
        jnp.zeros((tile_count, room_each, ray_count), jnp.int32)
        .at[owner_of, slot_of]
        .set(counts[0])
    )
    send_meta = (
        jnp.zeros((tile_count, room_each, 2), jnp.float32)
        .at[owner_of, slot_of]
        .set(jnp.stack([gains[0], brick_worth], axis=1))
    )
    got_bricks = lax.all_to_all(send_bricks, "tile", split_axis=0, concat_axis=0, tiled=True)
    got_counts = lax.all_to_all(send_counts, "tile", split_axis=0, concat_axis=0, tiled=True)
    got_meta = lax.all_to_all(
        send_meta.astype(jnp.bfloat16), "tile", split_axis=0, concat_axis=0, tiled=True
    ).astype(send_meta.dtype)
    senders = got_bricks.shape[0]
    items = got_bricks.shape[1]
    grade_of = level_from_worth(got_meta[:, :, 1]).reshape(senders * items)
    rendered = render(
        got_bricks.reshape(senders * items, brick_side, ray_count),
        grade_of,
        got_counts.reshape(senders * items, ray_count),
        got_meta[:, :, 0].reshape(senders * items),
        tf_slope,
        tent_rows,
        plane_maps,
        earlier_map,
    )
    rendered = rendered.reshape(senders, items, 4, ray_count)
    returned = lax.all_to_all(rendered, "tile", split_axis=0, concat_axis=0, tiled=True)
    load_sum = jnp.sum(got_meta[:, :, 1], axis=0, keepdims=True)
    returned, load_sum = (returned, load_sum)
    partials = returned[owner_of, slot_of]
    work_share = jnp.sum(load_sum) / held_bricks
    span_rows = held_bricks * ray_count // depth_count
    layered = jnp.transpose(partials, (1, 0, 2)).reshape(4, held_bricks * ray_count)
    layered = jnp.transpose(layered.reshape(4, span_rows, depth_count), (0, 2, 1))
    passing = layered[3]
    in_front = entering(passing, "depth", jnp.multiply, jnp.ones_like(passing))
    weighted = jnp.concatenate(
        [layered[:3] * in_front[None], (in_front * (1.0 - passing))[None]], axis=0
    )
    composite = lax.psum_scatter(weighted, "depth", scatter_dimension=1, tiled=True)
    return (composite, work_share.reshape(1, 1))


def solution(mesh):
    placed = (
        P("depth", "tile", None, None),
        P("depth", "tile"),
        P("depth", "tile", None),
        P("depth", "tile"),
        P("depth", None, None),
        P(),
    )
    return jax.shard_map(
        local,
        mesh=mesh,
        in_specs=placed,
        out_specs=(P(None, "depth", "tile"), P("depth", "tile")),
        check_vma=False,
    )
```

profile of v0, /device:TPU:1, one launch (start us, length us, event | category | flops | bytes accessed | tf_op | source)
XLA Modules:
  0.0 812.5 jit_solution(2389287067798779604)
XLA Ops:
  11.2 10.5 %all-to-all-start = ((bf16[32,1,2]{2,1,0:T(2,128)(2,1)}), bf16[32,1,2]{2,1,0:T(2,128)(2,1)S(1)}, u32[]{:S(2)}, u32[]{:S(2)}) async-start(bf16[32,1,2]{2,1,0:T(2,128)(2,1)} %copy.60), calls=%async_computation | async-start | bytes 32768 | tf_op jit(solution)/shard_map/all_to_all | solution.py:126
  23.2 7.1 all-to-all-done
  30.3 3.9 all-to-all-start.2
  38.8 4.6 all-to-all-done.2
  43.3 5.0 all-to-all-start.1
  50.6 45.6 %all-to-all-done.1 = bf16[32,1,32,1024]{3,2,1,0:T(8,128)(2,1)} async-done(((bf16[32,1,32,1024]{3,2,1,0:T(8,128)(2,1)}), bf16[32,1,32,1024]{3,2,1,0:T(8,128)(2,1)}, u32[]{:S(2)}, u32[]{:S(2)}) %all-to-all-start.1) | async-done | bytes 2097184 | tf_op jit(solution)/shard_map/all_to_all | solution.py:124
  96.2 449.7 %while.23 = (s32[]{:T(128)}, f32[32,4,1024]{2,1,0:T(4,128)S(1)}, s32[32]{0:T(128)S(1)}, bf16[32,32,1024]{2,1,0:T(8,128)(2,1)}, s32[32,1024]{1,0:T(8,128)S(1)}, /...) while((s32[]{:T(128)}, f32[32,4,1024]{2,1,0:T(4,128)S(1)}, ...), condition=%wide.region_18.19_spmd.clone.clone, body=%wide.region_4.18_spmd.clone.clone.sunk | while | flops 96355328 | bytes 10170007 | solution.py:83
  97.6 5.3 multiply_convert_fusion.8
  106.9 5.3 multiply_convert_fusion.8
  116.1 5.3 multiply_convert_fusion.8
  123.9 15.8 %conditional.4 = (f32[1,4,1024]{2,1,0:T(4,128)S(1)}) conditional(s32[]{:T(128)} %clamp.25, (f32[]{:T(128)}, s32[1024]{0:T(1024)S(1)}, bf16[32,1024]{1,0:T(8,128)(2,1)S(1)}, bf16[8,8,32,32]{3,2,1,0:T(8,128)(2,1)S(1)}, f32[]{:T(128)}, /*index=5*/f32[32,32]{1,0:T(8,128)S(1)}, f32[3]{0:T(128)S(1)}, ...), branch_computations={%region_5.8_spmd, %region_9.12_spmd, %region_13.16_spmd, %region_1... | conditional | flops 93600768 | bytes 7217332 | solution.py:81
  124.6 11.3 %convert_element_type.75 = bf16[1024,1024]{1,0:T(8,128)(2,1)S(1)} reshape(bf16[32,32,32,32]{3,2,1,0:T(8,128)(2,1)} %get-tuple-element.359) | data formatting | bytes 4194304 | tf_op jit(solution)/shard_map/convert_element_type | solution.py:95
  141.2 5.3 multiply_convert_fusion.8
  148.9 6.8 conditional.4
  157.2 5.3 multiply_convert_fusion.8
  165.0 6.8 conditional.4
  173.3 5.3 multiply_convert_fusion.8
  182.6 5.3 multiply_convert_fusion.8
  190.3 5.0 conditional.4
  196.8 5.3 multiply_convert_fusion.8
  204.5 5.0 conditional.4
  210.9 5.3 multiply_convert_fusion.8
  220.2 5.3 multiply_convert_fusion.8
  229.5 5.3 multiply_convert_fusion.8
  237.2 5.0 conditional.4
  243.7 5.3 multiply_convert_fusion.8
  251.4 6.8 conditional.4
  259.7 5.3 multiply_convert_fusion.8
  267.5 15.8 %conditional.4 = (f32[1,4,1024]{2,1,0:T(4,128)S(1)}) conditional(s32[]{:T(128)} %clamp.25, (f32[]{:T(128)}, s32[1024]{0:T(1024)S(1)}, bf16[32,1024]{1,0:T(8,128)(2,1)S(1)}, bf16[8,8,32,32]{3,2,1,0:T(8,128)(2,1)S(1)}, f32[]{:T(128)}, /*index=5*/f32[32,32]{1,0:T(8,128)S(1)}, f32[3]{0:T(128)S(1)}, ...), branch_computations={%region_5.8_spmd, %region_9.12_spmd, %region_13.16_spmd, %region_1... | conditional | flops 93600768 | bytes 7217332 | solution.py:81
  268.2 11.3 %convert_element_type.75 = bf16[1024,1024]{1,0:T(8,128)(2,1)S(1)} reshape(bf16[32,32,32,32]{3,2,1,0:T(8,128)(2,1)} %get-tuple-element.359) | data formatting | bytes 4194304 | tf_op jit(solution)/shard_map/convert_element_type | solution.py:95
  284.8 5.3 multiply_convert_fusion.8
  294.1 5.3 multiply_convert_fusion.8
  301.8 5.0 conditional.4
  308.3 5.3 multiply_convert_fusion.8
  317.5 5.3 multiply_convert_fusion.8
  326.8 5.3 multiply_convert_fusion.8
  334.5 15.8 %conditional.4 = (f32[1,4,1024]{2,1,0:T(4,128)S(1)}) conditional(s32[]{:T(128)} %clamp.25, (f32[]{:T(128)}, s32[1024]{0:T(1024)S(1)}, bf16[32,1024]{1,0:T(8,128)(2,1)S(1)}, bf16[8,8,32,32]{3,2,1,0:T(8,128)(2,1)S(1)}, f32[]{:T(128)}, /*index=5*/f32[32,32]{1,0:T(8,128)S(1)}, f32[3]{0:T(128)S(1)}, ...), branch_computations={%region_5.8_spmd, %region_9.12_spmd, %region_13.16_spmd, %region_1... | conditional | flops 93600768 | bytes 7217332 | solution.py:81
  335.2 11.3 %convert_element_type.75 = bf16[1024,1024]{1,0:T(8,128)(2,1)S(1)} reshape(bf16[32,32,32,32]{3,2,1,0:T(8,128)(2,1)} %get-tuple-element.359) | data formatting | bytes 4194304 | tf_op jit(solution)/shard_map/convert_element_type | solution.py:95
  351.8 5.3 multiply_convert_fusion.8
  361.1 5.3 multiply_convert_fusion.8
  368.8 5.0 conditional.4
  375.3 5.3 multiply_convert_fusion.8
  384.6 5.3 multiply_convert_fusion.8
  393.8 5.3 multiply_convert_fusion.8
  403.1 5.3 multiply_convert_fusion.8
  412.3 5.3 multiply_convert_fusion.8
  420.1 6.8 conditional.4
  428.4 5.3 multiply_convert_fusion.8
  436.2 6.8 conditional.4
  444.5 5.3 multiply_convert_fusion.8
  452.2 15.8 %conditional.4 = (f32[1,4,1024]{2,1,0:T(4,128)S(1)}) conditional(s32[]{:T(128)} %clamp.25, (f32[]{:T(128)}, s32[1024]{0:T(1024)S(1)}, bf16[32,1024]{1,0:T(8,128)(2,1)S(1)}, bf16[8,8,32,32]{3,2,1,0:T(8,128)(2,1)S(1)}, f32[]{:T(128)}, /*index=5*/f32[32,32]{1,0:T(8,128)S(1)}, f32[3]{0:T(128)S(1)}, ...), branch_computations={%region_5.8_spmd, %region_9.12_spmd, %region_13.16_spmd, %region_1... | conditional | flops 93600768 | bytes 7217332 | solution.py:81
  452.9 11.3 %convert_element_type.75 = bf16[1024,1024]{1,0:T(8,128)(2,1)S(1)} reshape(bf16[32,32,32,32]{3,2,1,0:T(8,128)(2,1)} %get-tuple-element.359) | data formatting | bytes 4194304 | tf_op jit(solution)/shard_map/convert_element_type | solution.py:95
  469.5 5.3 multiply_convert_fusion.8
  477.2 15.8 %conditional.4 = (f32[1,4,1024]{2,1,0:T(4,128)S(1)}) conditional(s32[]{:T(128)} %clamp.25, (f32[]{:T(128)}, s32[1024]{0:T(1024)S(1)}, bf16[32,1024]{1,0:T(8,128)(2,1)S(1)}, bf16[8,8,32,32]{3,2,1,0:T(8,128)(2,1)S(1)}, f32[]{:T(128)}, /*index=5*/f32[32,32]{1,0:T(8,128)S(1)}, f32[3]{0:T(128)S(1)}, ...), branch_computations={%region_5.8_spmd, %region_9.12_spmd, %region_13.16_spmd, %region_1... | conditional | flops 93600768 | bytes 7217332 | solution.py:81
  477.9 11.3 %convert_element_type.75 = bf16[1024,1024]{1,0:T(8,128)(2,1)S(1)} reshape(bf16[32,32,32,32]{3,2,1,0:T(8,128)(2,1)} %get-tuple-element.359) | data formatting | bytes 4194304 | tf_op jit(solution)/shard_map/convert_element_type | solution.py:95
  494.5 5.3 multiply_convert_fusion.8
  503.8 5.3 multiply_convert_fusion.8
  513.1 5.3 multiply_convert_fusion.8
  520.8 15.8 %conditional.4 = (f32[1,4,1024]{2,1,0:T(4,128)S(1)}) conditional(s32[]{:T(128)} %clamp.25, (f32[]{:T(128)}, s32[1024]{0:T(1024)S(1)}, bf16[32,1024]{1,0:T(8,128)(2,1)S(1)}, bf16[8,8,32,32]{3,2,1,0:T(8,128)(2,1)S(1)}, f32[]{:T(128)}, /*index=5*/f32[32,32]{1,0:T(8,128)S(1)}, f32[3]{0:T(128)S(1)}, ...), branch_computations={%region_5.8_spmd, %region_9.12_spmd, %region_13.16_spmd, %region_1... | conditional | flops 93600768 | bytes 7217332 | solution.py:81
  521.5 11.3 %convert_element_type.75 = bf16[1024,1024]{1,0:T(8,128)(2,1)S(1)} reshape(bf16[32,32,32,32]{3,2,1,0:T(8,128)(2,1)} %get-tuple-element.359) | data formatting | bytes 4194304 | tf_op jit(solution)/shard_map/convert_element_type | solution.py:95
  538.1 5.3 multiply_convert_fusion.8
  545.9 62.5 %all_to_all.20 = f32[32,1,4,1024]{3,2,1,0:T(4,128)S(1)} all-to-all(f32[32,1,4,1024]{3,2,1,0:T(4,128)S(1)} %bitcast.120), channel_id=1, replica_groups=mesh['depth'=16,'tile'=32] {'tile'}, dimensions={0} | all-to-all | bytes 1048576 | tf_op jit(solution)/shard_map/all_to_all | solution.py:143
  610.9 65.8 %all-gather.2.cloned.1.call-done = f32[16,16,1024]{2,1,0:T(8,128)} async-done(((f32[1,16,1024]{2,1,0:T(8,128)}), f32[16,16,1024]{2,1,0:T(8,128)}) %all-gather.2.cloned.1.call-update) | async-done | bytes 1048592 | tf_op jit(solution)/shard_map/all_gather | solution.py:9
  681.4 121.2 %all-reduce.3.cloned.1.call-done = f32[4,16,1024]{2,0,1:T(4,128)} async-done(((f32[4,16,1024]{2,0,1:T(4,128)}), f32[4,16,1024]{2,0,1:T(4,128)}) %all-reduce.3.cloned.1.call-update) | async-done | bytes 262160
  (604 shorter events, 190.5 us)
Async XLA Ops:
  7.2 14.6 %copy-start = (s32[1,16,1024]{2,1,0:T(8,128)S(1)}, s32[1,16,1024]{2,1,0:T(8,128)}, u32[]{:S(2)}) copy-start(s32[1,16,1024]{2,1,0:T(8,128)} %param.16) | copy-start | bytes 196612
  7.2 28.6 %copy-start.1 = (bf16[1,16,32,1024]{3,2,1,0:T(8,128)(2,1)S(1)}, bf16[1,16,32,1024]{3,2,1,0:T(8,128)(2,1)}, u32[]{:S(2)}) copy-start(bf16[1,16,32,1024]{3,2,1,0:T(8,128)(2,1)} %param.14) | copy-start | bytes 3145732
  11.2 19.1 %all-to-all-start = ((bf16[32,1,2]{2,1,0:T(2,128)(2,1)}), bf16[32,1,2]{2,1,0:T(2,128)(2,1)S(1)}, u32[]{:S(2)}, u32[]{:S(2)}) async-start(bf16[32,1,2]{2,1,0:T(2,128)(2,1)} %copy.60), calls=%async_computation | async-start | bytes 32768 | tf_op jit(solution)/shard_map/all_to_all | solution.py:126
  30.3 13.0 %all-to-all-start.2 = ((s32[32,1,1024]{2,1,0:T(1,128)}), s32[32,1,1024]{2,1,0:T(1,128)S(1)}, u32[]{:S(2)}, u32[]{:S(2)}) async-start(s32[32,1,1024]{2,1,0:T(1,128)} %reshape.262), calls=%async_computation.2 | async-start | bytes 262144 | tf_op jit(solution)/shard_map/all_to_all | solution.py:125
  43.3 52.9 %copy-start.2 = (f32[3]{0:T(128)S(1)}, f32[3]{0:T(128)}, u32[]{:S(2)}) copy-start(f32[3]{0:T(128)} %param.19) | copy-start | bytes 40
  43.3 52.9 %all-to-all-start.1 = ((bf16[32,1,32,1024]{3,2,1,0:T(8,128)(2,1)}), bf16[32,1,32,1024]{3,2,1,0:T(8,128)(2,1)}, u32[]{:S(2)}, u32[]{:S(2)}) async-start(bf16[32,1,32,1024]{3,2,1,0:T(8,128)(2,1)} %bitcast.34), calls=%async_computation.1 | async-start | bytes 4194304 | tf_op jit(solution)/shard_map/all_to_all | solution.py:124
  48.3 628.4 %all-gather.2.cloned.1.call-start = ((), (), s32[]{:S(2)}) async-start(), calls=%async_computation.4 | async-start | bytes 1114112 | tf_op jit(solution)/shard_map/all_gather | solution.py:9
  610.9 191.7 %all-reduce.3.cloned.1.call-start = ((), (), s32[]{:S(2)}) async-start(), calls=%async_computation.5 | async-start | bytes 524288
Sparse Core Ops, SparseCore 0:
  611.0 65.6 all-gather.1
  679.6 122.9 all-reduce.2
where the time goes:
time: 819 us; the launch traced here: 813 us
  waiting for transfers between devices  244 us (30%)
  other arithmetic  191 us (23%)
  local copies, waits for them, and re-layouts  177 us (22%)
  blocking collectives  62.5 us (8%)
  matrix products  56.7 us (7%)
  loops' own time  45.1 us (6%)
  starting transfers between devices  19.6 us (2%)
  between operations  16.1 us (2%)
    convert_element_type x96, other arithmetic, local(): plane_maps.append(jnp.kron(narrow, narrow).astype(jnp.bfloat16))  186 us
    unnamed x3, waiting for transfers between devices  121 us
    convert_element_type x16, local copies, waits for them, and re-layouts, local(): plane_maps.append(jnp.kron(narrow, narrow).astype(jnp.bfloat16))  82.2 us
    all_gather x1, waiting for transfers between devices, entering(): gathered = lax.all_gather(part, axis)  65.8 us
    all_to_all x1, blocking collectives, local(): lax.all_to_all(rendered, 'tile', split_axis=0, concat_axis=0, tiled=True)  62.5 us
    dot_general x16, matrix products, shade(): jnp.einsum('zs,sq->zq', earlier_map, optical, precision=highest)  47.3 us
    all_to_all x1, waiting for transfers between devices, local(): lax.all_to_all(send_bricks, 'tile', split_axis=0, concat_axis=0, tiled=True)  45.6 us
    another operation x1, loops' own time, render(): return lax.map(one_brick, (brick_data, grade_of, live_count, gain_of))  43.4 us
  transfers between devices with their start and end apart: 5, of which 5 were waited for; matrix products, arithmetic and copies ran while one was open for 1% of the time, Pallas kernels for 0%

commit v1 on v0

v1 whole, which is shorter than its diff:
```python
import functools

import jax
import jax.numpy as jnp
from jax import lax
from jax.experimental import pallas as pl
from jax.experimental.pallas import tpu as pltpu
from jax.sharding import PartitionSpec as P

F32 = jnp.float32
BF16 = jnp.bfloat16
I32 = jnp.int32
MESH = pl.DeviceIdType.MESH


def tent(at, cell):
    return jnp.maximum(0.0, 1.0 - jnp.abs(at - cell))


def coarse_at(fine, side):
    return jnp.clip((fine + 0.5) * (side / 32.0) - 0.5, 0.0, side - 1.0)


def fill_plane_maps(maps):
    lane = lax.broadcasted_iota(I32, (8, 1024), 1)
    y_of = (lane // 32).astype(F32)
    x_of = lax.broadcasted_iota(I32, (32, 128), 1) % 32
    e_of = lax.broadcasted_iota(I32, (32, 128), 0).astype(F32)
    for first, side in ((0, 8), (256, 16)):
        along_x = tent(coarse_at(x_of.astype(F32), side), e_of)
        along_x = jnp.concatenate([along_x] * 8, axis=1)
        y_at = coarse_at(y_of, side)

        def one(c, carry, first=first, along_x=along_x, y_at=y_at):
            along_y = tent(y_at, c.astype(F32))
            both = along_x * jnp.concatenate([along_y] * 4, axis=0)
            maps[pl.ds(pl.multiple_of(first + c * 32, 32), 32), :] = both.astype(BF16)
            return carry

        lax.fori_loop(0, side, one, 0)


def depth_map(levels, half):
    lane = lax.broadcasted_iota(I32, (1, 256), 1)
    slot = lane // 32
    grade = jnp.zeros((1, 256), I32)
    for s in range(8):
        grade = jnp.where(slot == s, levels[0, 2 * s + half], grade)
    side = jnp.where(grade == 2, 32.0, jnp.where(grade == 1, 16.0, 8.0))
    cell = lane % 32
    cell = jnp.where(grade == 2, cell, cell % 16).astype(F32)
    row = lax.broadcasted_iota(I32, (256, 256), 0)
    z_of = (row // 8).astype(F32)
    at = jnp.minimum(jnp.maximum((z_of + 0.5) * (side / 32.0) - 0.5, 0.0), side - 1.0)
    same = (row % 8) == (lax.broadcasted_iota(I32, (256, 256), 1) // 32)
    return jnp.where(same, tent(at, cell), 0.0).astype(BF16)


def kernel(
    depth_count, x_count, y_count,
    bricks, levels, counts, gains, owners, slope,
    out, share,
    raw, lives, masked, maps, cells, zmaps, dens, shaded, sends, boxes, mine, other,
    row_send, row_got, block_send, block_got,
    brick_sem, live_sem, send_sem, box_sem, pair_sem, row_sems, row_box, block_sems, block_box,
):
    me = lax.axis_index("depth")
    tile = lax.axis_index("tile")
    chip, core = me // 2, me % 2
    chips = depth_count // 2
    my_x, my_y = tile // y_count, tile % y_count

    fetch_bricks = [
        pltpu.make_async_copy(bricks.at[0, pl.ds(i * 8, 8)], raw.at[pl.ds(i * 8, 8)], brick_sem.at[i])
        for i in range(2)
    ]
    fetch_lives = [
        pltpu.make_async_copy(counts.at[0, :, pl.ds(j * 128, 128)], lives.at[j], live_sem.at[j])
        for j in range(8)
    ]
    for copy in fetch_bricks + fetch_lives:
        copy.start()

    barrier = pltpu.get_barrier_semaphore()

    def greet_depth(hop, carry):
        pl.semaphore_signal(barrier, inc=1, device_id={"depth": lax.rem(me + hop, depth_count)}, device_id_type=MESH)
        return carry

    lax.fori_loop(1, depth_count, greet_depth, 0)
    for hop in range(1, y_count):
        there = my_x * y_count + lax.rem(my_y + hop, y_count)
        pl.semaphore_signal(barrier, inc=1, device_id={"tile": there}, device_id_type=MESH)
    for hop in range(1, x_count):
        there = lax.rem(my_x + hop, x_count) * y_count + my_y
        pl.semaphore_signal(barrier, inc=1, device_id={"tile": there}, device_id_type=MESH)

    fill_plane_maps(maps)
    for half in range(2):
        zmaps[half] = depth_map(levels, half)

    for copy in fetch_bricks:
        copy.wait()
    for slot in range(16):
        b = 2 * (slot % 8) + slot // 8
        grade = levels[0, b]
        rows = pl.ds(slot * 16, 16)
        for first, width, wanted in ((0, 256, 0), (256, 512, 1)):
            keep = jnp.full((16, width), jnp.where(grade == wanted, 1.0, 0.0), F32).astype(BF16)
            masked[rows, first : first + width] = raw[b, 0:16, 0:width] * keep

    for n in range(4):
        lanes = pl.ds(n * 256, 256)
        plane = jnp.dot(masked[...], maps[:, lanes], preferred_element_type=F32)
        high = plane.astype(BF16)
        low = (plane - high.astype(F32)).astype(BF16)
        for slot in range(16):
            b = 2 * (slot % 8) + slot // 8
            keep = jnp.full((16, 256), jnp.where(levels[0, b] == 2, 1.0, 0.0), F32).astype(BF16)
            here = slice(slot * 16, slot * 16 + 16)
            cells[pl.ds(slot * 32, 16), lanes] = raw[b, 0:16, lanes] * keep + high[here]
            cells[pl.ds(slot * 32 + 16, 16), lanes] = raw[b, 16:32, lanes] * keep + low[here]

    for half in range(2):
        for n in range(4):
            lanes = pl.ds(n * 256, 256)
            dens[half, :, lanes] = jnp.dot(
                zmaps[half], cells[pl.ds(half * 256, 256), lanes], preferred_element_type=F32
            )

    pl.semaphore_wait(barrier, depth_count - 1 + y_count - 1 + x_count - 1)

    sub = lax.broadcasted_iota(I32, (8, 128), 0)
    lane = lax.broadcasted_iota(I32, (8, 128), 1)
    level_row = jnp.zeros((8, 128), I32)
    for b in range(16):
        level_row = jnp.where(lane == b, levels[0, b], level_row)
    row_send[...] = level_row
    row_got[my_y] = level_row
    row_copies = []
    for hop in range(1, y_count):
        there = my_x * y_count + lax.rem(my_y + hop, y_count)
        copy = pltpu.make_async_remote_copy(
            src_ref=row_send, dst_ref=row_got.at[my_y],
            send_sem=row_sems.at[hop], recv_sem=row_box.at[my_y],
            device_id={"tile": there}, device_id_type=MESH,
        )
        copy.start()
        row_copies.append(copy)

    for copy in fetch_lives:
        copy.wait()
    slopes = [slope[k] * 0.5 for k in range(3)]
    sends_started = []
    block_copies = []
    for half in range(2):
        gain = jnp.zeros((8, 128), F32)
        for s in range(8):
            gain = jnp.where(sub == s, -gains[0, 2 * s + half], gain)

        def shade(j, carry, half=half, gain=gain):
            lanes = pl.ds(pl.multiple_of(j * 128, 128), 128)
            live = lives[j, pl.ds(half, 8, stride=2), :]
            tau = jnp.zeros((8, 128), F32)
            through = jnp.ones((8, 128), F32)
            sums = [jnp.zeros((8, 128), F32)] * 3
            for z in range(32):
                x = dens[half, z * 8 : z * 8 + 8, lanes]
                soft = jnp.log(1.0 + jnp.exp(x))
                tau = tau + jnp.where(live > z, soft * gain, 0.0)
                after = jnp.exp(tau)
                glow = through - after
                through = after
                for k in range(3):
                    sums[k] = sums[k] + glow * jnp.tanh(x * slopes[k])
            solid = 1.0 - through
            for k in range(3):
                shaded[k, j] = 0.5 * (solid + sums[k])
            shaded[3, j] = through
            return carry

        lax.fori_loop(0, 8, shade, 0)

        source = (lane % 8) * 16 + (lane // 8 % 8) * 2 + lane // 64
        for k in range(4):
            parts = [
                jnp.take_along_axis(shaded[k, j], source, axis=1, mode="promise_in_bounds")
                for j in range(8)
            ]
            for bit in range(3):
                step = 1 << bit
                upper = (lane // (8 * step)) % 2 == 1
                for j in range(8):
                    if j & step:
                        continue
                    a, b = parts[j], parts[j + step]
                    parts[j] = jnp.where(upper, pltpu.roll(b, 8 * step, 1), a)
                    parts[j + step] = jnp.where(upper, b, pltpu.roll(a, 128 - 8 * step, 1))
            for g in range(8):
                sends[half, g, k] = parts[g]

        for hop in (4, 3, 5, 2, 6, 1, 7):
            to = lax.rem(chip + hop, chips)
            copy = pltpu.make_async_remote_copy(
                src_ref=sends.at[half, to], dst_ref=boxes.at[me],
                send_sem=send_sem.at[half, hop], recv_sem=box_sem.at[me],
                device_id={"depth": 2 * to + half}, device_id_type=MESH,
            )
            copy.start()
            sends_started.append(copy)

        @pl.when(core == half)
        def _(half=half):
            pltpu.make_async_copy(sends.at[half, chip], boxes.at[me], box_sem.at[me]).start()

        @pl.when(core != half)
        def _(half=half):
            pltpu.make_async_remote_copy(
                src_ref=sends.at[half, chip], dst_ref=boxes.at[me],
                send_sem=send_sem.at[0, 0], recv_sem=box_sem.at[me],
                device_id={"depth": 2 * chip + half}, device_id_type=MESH,
            ).start()

        if half == 0:
            for hop in range(1, y_count):
                there = lax.rem(my_y + y_count - hop, y_count)
                pltpu.make_async_copy(row_got.at[there], row_got.at[there], row_box.at[there]).wait()
            block = jnp.zeros((8, 128), I32)
            for y in range(y_count):
                block = jnp.where(sub == y, row_got[y], block)
            block_send[...] = block
            block_got[my_x] = block
            for hop in range(1, x_count):
                there = lax.rem(my_x + hop, x_count) * y_count + my_y
                copy = pltpu.make_async_remote_copy(
                    src_ref=block_send, dst_ref=block_got.at[my_x],
                    send_sem=block_sems.at[hop], recv_sem=block_box.at[my_x],
                    device_id={"tile": there}, device_id_type=MESH,
                )
                copy.start()
                block_copies.append(copy)

    for hop in range(1, x_count):
        there = lax.rem(my_x + x_count - hop, x_count)
        pltpu.make_async_copy(block_got.at[there], block_got.at[there], block_box.at[there]).wait()
    total = jnp.zeros((y_count, 16), F32)
    for x in range(x_count):
        grade = block_got[x][0:y_count, 0:16]
        worth = jnp.where(grade == 2, 1.0, jnp.where(grade == 1, 0.25, 0.0625))
        total = total + jnp.where(owners[0, x * y_count : (x + 1) * y_count] == tile, worth, 0.0)
    share[...] = jnp.sum(total, keepdims=True) * (1.0 / 16.0)

    through = jnp.ones((8, 128), F32)
    colors = [jnp.zeros((8, 128), F32)] * 3
    for d in range(depth_count):
        pltpu.make_async_copy(boxes.at[d], boxes.at[d], box_sem.at[d]).wait()
        for k in range(3):
            colors[k] = colors[k] + through * boxes[d, k]
        through = through * boxes[d, 3]
    final = colors + [1.0 - through]
    for k in range(4):
        mine[k] = final[k]
    swap = pltpu.make_async_remote_copy(
        src_ref=mine, dst_ref=other, send_sem=pair_sem.at[0], recv_sem=pair_sem.at[1],
        device_id={"depth": me + 1 - 2 * core}, device_id_type=MESH,
    )
    swap.start()
    for copy in sends_started + row_copies + block_copies:
        copy.wait_send()
    pltpu.make_async_remote_copy(
        src_ref=sends.at[0, 0], dst_ref=boxes.at[me],
        send_sem=send_sem.at[0, 0], recv_sem=box_sem.at[me],
        device_id={"depth": me + 1 - 2 * core}, device_id_type=MESH,
    ).wait_send()
    swap.wait()
    keep = (lane // 64) == core
    for k in range(4):
        out[k] = jnp.where(keep, final[k], pltpu.roll(other[k], 64, 1))


def local(bricks, levels, counts, gains, ownership, tf_slope):
    depth_count = lax.axis_size("depth")
    tile_count = lax.axis_size("tile")
    y_count = min(8, tile_count)
    x_count = tile_count // y_count
    vmem = pl.BlockSpec(memory_space=pltpu.VMEM)
    smem = pl.BlockSpec(memory_space=pltpu.SMEM)
    anywhere = pl.BlockSpec(memory_space=pl.ANY)
    dma = pltpu.SemaphoreType.DMA
    composite, share = pl.pallas_call(
        functools.partial(kernel, depth_count, x_count, y_count),
        out_shape=(
            jax.ShapeDtypeStruct((4, 8, 128), F32),
            jax.ShapeDtypeStruct((1, 1), F32),
        ),
        in_specs=[anywhere, smem, anywhere, smem, vmem, smem],
        out_specs=(vmem, vmem),
        scratch_shapes=[
            pltpu.VMEM((16, 32, 1024), BF16),
            pltpu.VMEM((8, 16, 128), I32),
            pltpu.VMEM((256, 768), BF16),
            pltpu.VMEM((768, 1024), BF16),
            pltpu.VMEM((512, 1024), BF16),
            pltpu.VMEM((2, 256, 256), BF16),
            pltpu.VMEM((2, 256, 1024), F32),
            pltpu.VMEM((4, 8, 8, 128), F32),
            pltpu.VMEM((2, 8, 4, 8, 128), F32),
            pltpu.VMEM((16, 4, 8, 128), F32),
            pltpu.VMEM((4, 8, 128), F32),
            pltpu.VMEM((4, 8, 128), F32),
            pltpu.VMEM((8, 128), I32),
            pltpu.VMEM((8, 8, 128), I32),
            pltpu.VMEM((8, 128), I32),
            pltpu.VMEM((4, 8, 128), I32),
            dma((2,)),
            dma((8,)),
            dma((2, 8)),
            dma((16,)),
            dma((2,)),
            dma((8,)),
            dma((8,)),
            dma((4,)),
            dma((4,)),
        ],
        compiler_params=pltpu.CompilerParams(
            collective_id=0, has_side_effects=True, vmem_limit_bytes=40 * 1024 * 1024
        ),
        name="render",
    )(bricks, levels, counts, gains, ownership, tf_slope)
    return composite.reshape(4, 1, 1024), share


def solution(mesh):
    placed = (
        P("depth", "tile", None, None),
        P("depth", "tile"),
        P("depth", "tile", None),
        P("depth", "tile"),
        P("depth", None, None),
        P(),
    )
    return jax.shard_map(
        local,
        mesh=mesh,
        in_specs=placed,
        out_specs=(P(None, "depth", "tile"), P("depth", "tile")),
        check_vma=False,
    )
```

time: 819 us -> 34.6 us (0.04)
  waiting for transfers between devices: 244 us -> 0 us
  other arithmetic: 191 us -> 0 us
  local copies, waits for them, and re-layouts: 177 us -> 3.47 us
  blocking collectives: 62.5 us -> 0 us
  matrix products: 56.7 us -> 0 us
  loops' own time: 45.1 us -> 0 us
  Pallas kernels: 0 us -> 28.5 us
  starting transfers between devices: 19.6 us -> 0 us
  between operations: 16.1 us -> 2.37 us
    convert_element_type x130 -> x0, other arithmetic: 186 us -> none  [the longest x96 186 us: local(): plane_maps.append(jnp.kron(narrow, narrow).astype(jnp.bfloat16))]
    unnamed x3 -> x0, waiting for transfers between devices: 121 us -> none
    convert_element_type x17 -> x0, local copies, waits for them, and re-layouts: 82.9 us -> none  [the longest x16 82.2 us: local(): plane_maps.append(jnp.kron(narrow, narrow).astype(jnp.bfloat16))]
    all_gather x1 -> x0, waiting for transfers between devices: 65.8 us -> none  [entering(): gathered = lax.all_gather(part, axis)]
    all_to_all x1 -> x0, blocking collectives: 62.5 us -> none  [local(): lax.all_to_all(rendered, 'tile', split_axis=0, concat_axis=0, tiled=True)]
    all_to_all x3 -> x0, waiting for transfers between devices: 57.3 us -> none  [the longest x1 45.6 us: local(): lax.all_to_all(send_bricks, 'tile', split_axis=0, concat_axis=0, tiled=True)]
    dot_general x48 -> x0, matrix products: 56.7 us -> none  [the longest x16 47.3 us: shade(): jnp.einsum('zs,sq->zq', earlier_map, optical, precision=highest)]
    another operation x34 -> x0, loops' own time: 45.1 us -> none  [the longest x1 43.4 us: render(): return lax.map(one_brick, (brick_data, grade_of, live_count, gain_of))]
  transfers between devices with their start and end apart: 5 -> 0, of which waited for: 5 -> 0; matrix products, arithmetic and copies ran while one was open for 1% -> 0% of each run, Pallas kernels for 0% -> 0%
where the time goes in v1:
time: 34.6 us; the launch traced here: 34.3 us
  Pallas kernels  28.5 us (82%)
  local copies, waits for them, and re-layouts  3.47 us (10%)
  between operations  2.37 us (7%)
    pallas_call x1, Pallas kernels, local(): pl.pallas_call(functools.partial(kernel, depth_count, x_count, y_count),...  28.5 us
    unnamed x12, local copies, waits for them, and re-layouts  3.47 us

profile of v1, /device:TPU:1, one launch (start us, length us, event | category | flops | bytes accessed | tf_op | source)
XLA Modules:
  0.0 34.3 jit_solution(10543171303554709799)
XLA Ops:
  0.6 0.0 copy-start.4
  0.6 0.0 copy-start.3
  0.7 0.0 copy-start.2
  0.7 0.8 %copy.8.owners = s32[1,32,16]{2,1,0:T(8,128)S(1)} copy(s32[1,32,16]{1,2,0:T(8,128)} %param.10) | data formatting | bytes 4096 | tf_op args[4]
  1.4 0.0 copy-done.4
  1.5 0.0 copy-done.3
  1.5 0.0 copy-done.2
  1.5 0.0 copy-start
  1.5 1.2 %copy-done = bf16[1,16,32,1024]{3,2,1,0:T(8,128)(2,1)S(1)} copy-done((bf16[1,16,32,1024]{3,2,1,0:T(8,128)(2,1)S(1)}, bf16[1,16,32,1024]{3,2,1,0:T(8,128)(2,1)}, u32[]{:S(2)}) %copy-start) | copy-done | bytes 1048600
  2.7 0.0 copy-start.1
  2.7 0.8 %copy-done.1 = s32[1,16,1024]{2,1,0:T(8,128)S(1)} copy-done((s32[1,16,1024]{2,1,0:T(8,128)S(1)}, s32[1,16,1024]{2,1,0:T(8,128)}, u32[]{:S(2)}) %copy-start.1) | copy-done | bytes 65560
  3.5 28.5 %render.1 = (f32[4,8,128]{2,1,0:T(8,128)S(1)}, f32[1,1]{1,0:T(1,128)}) custom-call(bf16[1,16,32,1024]{3,2,1,0:T(8,128)(2,1)S(1)} %copy-done, s32[1,16]{1,0:T(1,128)S(1)} %copy-done.2, s32[1,16,1024]{2,1,0:T(8,128)S(1)} %copy-done.1, f32[1,16]{1,0:T(1,128)S(1)} %copy-done.3, s32[1,32,16]{2,1,0:T(8,128)S(1)} %copy.8.owners, f32[3]{0:T(128)S(1)} %copy-done.4), custom_call_target="tpu_custom_call" | custom-call | tf_op jit(solution)/shard_map/render/pallas_call | solution.py:290
  32.0 0.6 %copy.12 = f32[4,1,1024]{2,1,0:T(1,128)} copy(f32[4,1,1024]{2,1,0:T(1,128)S(1)} %bitcast.1) | data formatting | bytes 32768
Async XLA Ops:
  0.6 0.8 %copy-start.4 = (f32[3]{0:T(128)S(1)}, f32[3]{0:T(128)}, u32[]{:S(2)}) copy-start(f32[3]{0:T(128)} %slope.1) | copy-start | bytes 40
  0.6 0.8 %copy-start.3 = (f32[1,16]{1,0:T(1,128)S(1)}, f32[1,16]{1,0:T(1,128)}, u32[]{:S(2)}) copy-start(f32[1,16]{1,0:T(1,128)} %gains.1) | copy-start | bytes 196
  0.7 0.8 %copy-start.2 = (s32[1,16]{1,0:T(1,128)S(1)}, s32[1,16]{1,0:T(1,128)}, u32[]{:S(2)}) copy-start(s32[1,16]{1,0:T(1,128)} %levels.1) | copy-start | bytes 196
  1.5 1.2 %copy-start = (bf16[1,16,32,1024]{3,2,1,0:T(8,128)(2,1)S(1)}, bf16[1,16,32,1024]{3,2,1,0:T(8,128)(2,1)}, u32[]{:S(2)}) copy-start(bf16[1,16,32,1024]{3,2,1,0:T(8,128)(2,1)} %bricks.1) | copy-start | bytes 3145732
  2.7 0.8 %copy-start.1 = (s32[1,16,1024]{2,1,0:T(8,128)S(1)}, s32[1,16,1024]{2,1,0:T(8,128)}, u32[]{:S(2)}) copy-start(s32[1,16,1024]{2,1,0:T(8,128)} %counts.1) | copy-start | bytes 196612

commit v2 on v1

v2 whole, which is shorter than its diff:
```python
import functools

import jax
import jax.numpy as jnp
from jax import lax
from jax.experimental import pallas as pl
from jax.experimental.pallas import tpu as pltpu
from jax.sharding import PartitionSpec as P

F32 = jnp.float32
BF16 = jnp.bfloat16
I32 = jnp.int32
MESH = pl.DeviceIdType.MESH


def tent(at, cell):
    return jnp.maximum(0.0, 1.0 - jnp.abs(at - cell))


def coarse_at(fine, side):
    return jnp.clip((fine + 0.5) * (side / 32.0) - 0.5, 0.0, side - 1.0)


def fill_plane_maps(maps):
    lane = lax.broadcasted_iota(I32, (8, 1024), 1)
    y_of = (lane // 32).astype(F32)
    x_of = lax.broadcasted_iota(I32, (32, 128), 1) % 32
    e_of = lax.broadcasted_iota(I32, (32, 128), 0).astype(F32)
    for first, side in ((0, 8), (256, 16)):
        along_x = tent(coarse_at(x_of.astype(F32), side), e_of)
        along_x = jnp.concatenate([along_x] * 8, axis=1)
        y_at = coarse_at(y_of, side)

        def one(c, carry, first=first, along_x=along_x, y_at=y_at):
            along_y = tent(y_at, c.astype(F32))
            both = along_x * jnp.concatenate([along_y] * 4, axis=0)
            maps[pl.ds(pl.multiple_of(first + c * 32, 32), 32), :] = both.astype(BF16)
            return carry

        lax.fori_loop(0, side, one, 0)


def brick_of(slot):
    half, place = slot // 8, slot % 8
    return 8 * half + 2 * (place % 4) + place // 4


def depth_map(levels, half):
    lane = lax.broadcasted_iota(I32, (1, 256), 1)
    slot = lane // 32
    grade = jnp.zeros((1, 256), I32)
    for s in range(8):
        grade = jnp.where(slot == s, levels[0, brick_of(8 * half + s)], grade)
    side = jnp.where(grade == 2, 32.0, jnp.where(grade == 1, 16.0, 8.0))
    cell = lane % 32
    cell = jnp.where(grade == 2, cell, cell % 16).astype(F32)
    row = lax.broadcasted_iota(I32, (256, 256), 0)
    z_of = (row // 8).astype(F32)
    at = jnp.minimum(jnp.maximum((z_of + 0.5) * (side / 32.0) - 0.5, 0.0), side - 1.0)
    same = (row % 8) == (lax.broadcasted_iota(I32, (256, 256), 1) // 32)
    return jnp.where(same, tent(at, cell), 0.0).astype(BF16)


def kernel(
    depth_count, x_count, y_count,
    bricks, levels_in, counts, gains_in, owners_in, slope_in,
    out, share,
    levels, gains, slope, owners,
    raw, lives, masked, maps, cells, zmaps, dens, shaded, sends, boxes,
    col_send, col_got, block_send, block_got,
    small_sem, brick_sem, live_sem, send_sem, box_sem, col_sems, col_box, block_sems, block_box,
):
    me = lax.axis_index("depth")
    tile = lax.axis_index("tile")
    my_x, my_y = tile // y_count, tile % y_count

    fetch_small = [
        pltpu.make_async_copy(there, here, small_sem.at[i])
        for i, (there, here) in enumerate(
            ((levels_in, levels), (gains_in, gains), (slope_in, slope), (owners_in.at[0], owners))
        )
    ]
    fetch_bricks = [
        pltpu.make_async_copy(bricks.at[0, pl.ds(i * 4, 4)], raw.at[pl.ds(i * 4, 4)], brick_sem.at[i])
        for i in range(4)
    ]
    fetch_lives = [
        pltpu.make_async_copy(counts.at[0, :, pl.ds(j * 128, 128)], lives.at[j], live_sem.at[j])
        for j in range(8)
    ]
    for copy in fetch_small + fetch_bricks + fetch_lives:
        copy.start()

    barrier = pltpu.get_barrier_semaphore()

    def greet_depth(hop, carry):
        pl.semaphore_signal(barrier, inc=1, device_id={"depth": lax.rem(me + hop, depth_count)}, device_id_type=MESH)
        return carry

    lax.fori_loop(1, depth_count, greet_depth, 0)
    for hop in range(1, y_count):
        there = my_x * y_count + lax.rem(my_y + hop, y_count)
        pl.semaphore_signal(barrier, inc=1, device_id={"tile": there}, device_id_type=MESH)
    for hop in range(1, x_count):
        there = lax.rem(my_x + hop, x_count) * y_count + my_y
        pl.semaphore_signal(barrier, inc=1, device_id={"tile": there}, device_id_type=MESH)

    fill_plane_maps(maps)
    for copy in fetch_small:
        copy.wait()
    for half in range(2):
        zmaps[half] = depth_map(levels, half)

    for copy in fetch_bricks:
        copy.wait()
    for slot in range(16):
        b = brick_of(slot)
        grade = levels[0, b]
        rows = pl.ds(slot * 16, 16)
        for first, width, wanted in ((0, 256, 0), (256, 512, 1)):
            keep = jnp.full((16, width), jnp.where(grade == wanted, 1.0, 0.0), F32).astype(BF16)
            masked[rows, first : first + width] = raw[b, 0:16, 0:width] * keep

    for n in range(4):
        lanes = pl.ds(n * 256, 256)
        plane = jnp.dot(masked[...], maps[:, lanes], preferred_element_type=F32)
        high = plane.astype(BF16)
        low = (plane - high.astype(F32)).astype(BF16)
        for slot in range(16):
            b = brick_of(slot)
            keep = jnp.full((16, 256), jnp.where(levels[0, b] == 2, 1.0, 0.0), F32).astype(BF16)
            here = slice(slot * 16, slot * 16 + 16)
            cells[pl.ds(slot * 32, 16), lanes] = raw[b, 0:16, lanes] * keep + high[here]
            cells[pl.ds(slot * 32 + 16, 16), lanes] = raw[b, 16:32, lanes] * keep + low[here]

    for half in range(2):
        for n in range(4):
            lanes = pl.ds(n * 256, 256)
            dens[half, :, lanes] = jnp.dot(
                zmaps[half], cells[pl.ds(half * 256, 256), lanes], preferred_element_type=F32
            )

    sub = lax.broadcasted_iota(I32, (8, 128), 0)
    lane = lax.broadcasted_iota(I32, (8, 128), 1)
    for copy in fetch_lives:
        copy.wait()
    slopes = [slope[k] * 0.5 for k in range(3)]
    copies = []

    def share_columns():
        column = lax.broadcasted_iota(I32, (16, 128), 0)
        values = jnp.zeros((16, 128), I32)
        for b in range(16):
            values = jnp.where(column == b, levels[0, b], values)
        col_send[...] = values
        col_got[my_y] = values
        for hop in range(1, y_count):
            there = my_x * y_count + lax.rem(my_y + hop, y_count)
            copy = pltpu.make_async_remote_copy(
                src_ref=col_send, dst_ref=col_got.at[my_y],
                send_sem=col_sems.at[hop], recv_sem=col_box.at[my_y],
                device_id={"tile": there}, device_id_type=MESH,
            )
            copy.start()
            copies.append(copy)

    for half in range(2):
        gain = jnp.zeros((8, 128), F32)
        for s in range(8):
            gain = jnp.where(sub == s, -gains[0, brick_of(8 * half + s)], gain)

        def shade(j, carry, half=half, gain=gain):
            lanes = pl.ds(pl.multiple_of(j * 128, 128), 128)
            live = jnp.concatenate(
                [lives[j, pl.ds(8 * half + odd, 4, stride=2), :] for odd in range(2)], axis=0
            )
            tau = jnp.zeros((8, 128), F32)
            through = jnp.ones((8, 128), F32)
            sums = [jnp.zeros((8, 128), F32)] * 3
            for z in range(32):
                x = dens[half, z * 8 : z * 8 + 8, lanes]
                soft = jnp.log(1.0 + jnp.exp(x))
                tau = tau + jnp.where(live > z, soft * gain, 0.0)
                after = jnp.exp(tau)
                glow = through - after
                through = after
                for k in range(3):
                    sums[k] = sums[k] + glow * jnp.tanh(x * slopes[k])
            solid = 1.0 - through
            for k in range(3):
                shaded[k, j] = 0.5 * (solid + sums[k])
            shaded[3, j] = through
            return carry

        lax.fori_loop(0, 8, shade, 0)

        source = (lane % 8) * 16 + (lane // 8 % 8) * 2 + lane // 64
        own_side = (lane // 64) == (sub // 4)
        for pair in range(2):
            sorted_lanes = []
            for k in (2 * pair, 2 * pair + 1):
                parts = [
                    jnp.take_along_axis(shaded[k, j], source, axis=1, mode="promise_in_bounds")
                    for j in range(8)
                ]
                for bit in range(3):
                    step = 1 << bit
                    upper = (lane // (8 * step)) % 2 == 1
                    for j in range(8):
                        if j & step:
                            continue
                        a, b = parts[j], parts[j + step]
                        parts[j] = jnp.where(upper, pltpu.roll(b, 8 * step, 1), a)
                        parts[j + step] = jnp.where(upper, b, pltpu.roll(a, 128 - 8 * step, 1))
                sorted_lanes.append(
                    [jnp.where(own_side, v, pltpu.roll(pltpu.roll(v, 64, 1), 4, 0)) for v in parts]
                )
            for g in range(8):
                first, second = sorted_lanes[0][g], sorted_lanes[1][g]
                sends[half, 2 * g, pair] = jnp.where(sub < 4, first, pltpu.roll(second, 4, 0))
                sends[half, 2 * g + 1, pair] = jnp.where(sub < 4, pltpu.roll(first, 4, 0), second)

        if half == 0:
            pl.semaphore_wait(barrier, depth_count - 1 + y_count - 1 + x_count - 1)
        for hop in (8, 7, 9, 6, 10, 5, 11, 4, 12, 3, 13, 2, 14, 1, 15):
            to = lax.rem(me + hop, depth_count)
            copy = pltpu.make_async_remote_copy(
                src_ref=sends.at[half, to], dst_ref=boxes.at[half, me],
                send_sem=send_sem.at[half, hop], recv_sem=box_sem.at[half, me],
                device_id={"depth": to}, device_id_type=MESH,
            )
            copy.start()
            copies.append(copy)
        boxes[half, me] = sends[half, me]
        if half == 0:
            share_columns()

    lane16 = lax.broadcasted_iota(I32, (16, 128), 1)
    for hop in range(1, y_count):
        there = lax.rem(my_y + hop, y_count)
        pltpu.make_async_copy(col_got.at[there], col_got.at[there], col_box.at[there]).wait()
    block = jnp.zeros((16, 128), I32)
    for y in range(y_count):
        block = jnp.where(lane16 % y_count == y, col_got[y], block)
    block_send[...] = block
    block_got[my_x] = block
    for hop in range(1, x_count):
        there = lax.rem(my_x + hop, x_count) * y_count + my_y
        copy = pltpu.make_async_remote_copy(
            src_ref=block_send, dst_ref=block_got.at[my_x],
            send_sem=block_sems.at[hop], recv_sem=block_box.at[my_x],
            device_id={"tile": there}, device_id_type=MESH,
        )
        copy.start()
        copies.append(copy)
    for hop in range(1, x_count):
        there = lax.rem(my_x + hop, x_count)
        pltpu.make_async_copy(block_got.at[there], block_got.at[there], block_box.at[there]).wait()
    grade = jnp.zeros((16, 128), I32)
    for x in range(x_count):
        grade = jnp.where(lane16 // y_count == x, block_got[x], grade)
    grade = grade[:, 0 : x_count * y_count]
    worth = jnp.where(grade == 2, 1.0, jnp.where(grade == 1, 0.25, 0.0625))
    share[...] = jnp.sum(jnp.where(owners[...] == tile, worth, 0.0), keepdims=True) * (1.0 / 16.0)

    through = []
    colors = []
    for half in range(2):
        for hop in range(1, depth_count):
            frm = lax.rem(me + hop, depth_count)
            pltpu.make_async_copy(boxes.at[half, frm], boxes.at[half, frm], box_sem.at[half, frm]).wait()
        ahead = jnp.ones((8, 128), F32)
        sums = [jnp.zeros((8, 128), F32)] * 2
        for d in range(depth_count):
            first, second = boxes[half, d, 0], boxes[half, d, 1]
            sums = [sums[0] + ahead * first, sums[1] + ahead * second]
            ahead = ahead * jnp.where(sub < 4, pltpu.roll(second, 4, 0), second)
        through.append(ahead)
        colors.append(sums)
    low = sub < 4
    out[0] = jnp.where(low, colors[0][0], pltpu.roll(colors[1][0], 4, 0))
    out[1] = jnp.where(low, pltpu.roll(colors[0][0], 4, 0), colors[1][0])
    out[2] = jnp.where(low, colors[0][1], pltpu.roll(colors[1][1], 4, 0))
    out[3] = 1.0 - jnp.where(low, through[0], through[1])
    for copy in copies:
        copy.wait_send()


def local(bricks, levels, counts, gains, ownership, tf_slope):
    depth_count = lax.axis_size("depth")
    tile_count = lax.axis_size("tile")
    y_count = min(8, tile_count)
    x_count = tile_count // y_count
    vmem = pl.BlockSpec(memory_space=pltpu.VMEM)
    anywhere = pl.BlockSpec(memory_space=pl.ANY)
    dma = pltpu.SemaphoreType.DMA
    composite, share = pl.pallas_call(
        functools.partial(kernel, depth_count, x_count, y_count),
        out_shape=(
            jax.ShapeDtypeStruct((4, 8, 128), F32),
            jax.ShapeDtypeStruct((1, 1), F32),
        ),
        in_specs=[anywhere] * 6,
        out_specs=(vmem, vmem),
        scratch_shapes=[
            pltpu.SMEM((1, 16), I32),
            pltpu.SMEM((1, 16), F32),
            pltpu.SMEM((3,), F32),
            pltpu.VMEM((16, tile_count), I32),
            pltpu.VMEM((16, 32, 1024), BF16),
            pltpu.VMEM((8, 16, 128), I32),
            pltpu.VMEM((256, 768), BF16),
            pltpu.VMEM((768, 1024), BF16),
            pltpu.VMEM((512, 1024), BF16),
            pltpu.VMEM((2, 256, 256), BF16),
            pltpu.VMEM((2, 256, 1024), F32),
            pltpu.VMEM((4, 8, 8, 128), F32),
            pltpu.VMEM((2, 16, 2, 8, 128), F32),
            pltpu.VMEM((2, 16, 2, 8, 128), F32),
            pltpu.VMEM((16, 128), I32),
            pltpu.VMEM((8, 16, 128), I32),
            pltpu.VMEM((16, 128), I32),
            pltpu.VMEM((4, 16, 128), I32),
            dma((4,)),
            dma((4,)),
            dma((8,)),
            dma((2, 16)),
            dma((2, 16)),
            dma((8,)),
            dma((8,)),
            dma((4,)),
            dma((4,)),
        ],
        compiler_params=pltpu.CompilerParams(
            collective_id=0, has_side_effects=True, vmem_limit_bytes=60 * 1024 * 1024
        ),
        name="render",
    )(bricks, levels, counts, gains, jnp.swapaxes(ownership, 1, 2), tf_slope)
    return composite.reshape(4, 1, 1024), share


def solution(mesh):
    placed = (
        P("depth", "tile", None, None),
        P("depth", "tile"),
        P("depth", "tile", None),
        P("depth", "tile"),
        P("depth", None, None),
        P(),
    )
    return jax.shard_map(
        local,
        mesh=mesh,
        in_specs=placed,
        out_specs=(P(None, "depth", "tile"), P("depth", "tile")),
        check_vma=False,
    )
```

time: 34.6 us -> 28.4 us (0.82)
  Pallas kernels: 28.5 us -> 24.4 us
  local copies, waits for them, and re-layouts: 3.47 us -> 1.32 us
    pallas_call x1, Pallas kernels: 28.5 us -> 24.4 us  [local(): pl.pallas_call(functools.partial(kernel, depth_count, x_count, y_count),...]
    unnamed x12 -> x1, local copies, waits for them, and re-layouts: 3.47 us -> 1.32 us
where the time goes in v2:
time: 28.4 us; the launch traced here: 28.1 us
  Pallas kernels  24.4 us (86%)
  between operations  2.4 us (8%)
  local copies, waits for them, and re-layouts  1.32 us (5%)
    pallas_call x1, Pallas kernels, local(): pl.pallas_call(functools.partial(kernel, depth_count, x_count, y_count),...  24.4 us
    unnamed x1, local copies, waits for them, and re-layouts  1.32 us

profile of v2, /device:TPU:1, one launch (start us, length us, event | category | flops | bytes accessed | tf_op | source)
XLA Modules:
  0.0 28.1 jit_solution(17356490059064960675)
XLA Ops:
  0.6 24.4 %render.1 = (f32[4,8,128]{2,1,0:T(8,128)}, f32[1,1]{1,0:T(1,128)}) custom-call(bf16[1,16,32,1024]{3,2,1,0:T(8,128)(2,1)} %bricks.1, s32[1,16]{1,0:T(1,128)} %levels_in.1, s32[1,16,1024]{2,1,0:T(8,128)} %counts.1, f32[1,16]{1,0:T(1,128)} %gains_in.1, s32[1,16,32]{2,1,0:T(8,128)} %bitcast.3, f32[3]{0:T(128)} %slope_in.1), custom_call_target="tpu_custom_call" | custom-call | tf_op jit(solution)/shard_map/render/pallas_call | solution.py:297
  25.1 1.3 %copy.11 = f32[4,1,1024]{2,1,0:T(1,128)} copy(f32[4,1,1024]{2,1,0:T(1,128)} %bitcast.2) | data formatting | bytes 32768

commit v3 on v2

--- a/solution.py
+++ b/solution.py
@@ -11,6 +11,8 @@
 BF16 = jnp.bfloat16
 I32 = jnp.int32
 MESH = pl.DeviceIdType.MESH
+CODE_FLOOR = -20.75
+CODE_SCALE = 65535.0 / 23.75
 
 
 def tent(at, cell):
@@ -61,18 +63,31 @@
     return jnp.where(same, tent(at, cell), 0.0).astype(BF16)
 
 
+def encode(tau, solid, sums):
+    scale = 32767.5 / jnp.maximum(solid, 1e-12)
+    codes = [
+        jnp.clip(sums[k] * scale + 32768.0, 0.0, 65535.0).astype(I32) for k in range(3)
+    ]
+    depth = jnp.log2(jnp.maximum(-tau, 1e-12))
+    codes.append(jnp.clip((depth - CODE_FLOOR) * CODE_SCALE + 0.5, 0.0, 65535.0).astype(I32))
+    return codes[0] | (codes[1] << 16), codes[2] | (codes[3] << 16)
+
+
 def kernel(
     depth_count, x_count, y_count,
     bricks, levels_in, counts, gains_in, owners_in, slope_in,
-    out, share,
+    boxes, share,
     levels, gains, slope, owners,
-    raw, lives, masked, maps, cells, zmaps, dens, shaded, sends, boxes,
-    col_send, col_got, block_send, block_got,
-    small_sem, brick_sem, live_sem, send_sem, box_sem, col_sems, col_box, block_sems, block_box,
+    raw, lives, masked, maps, cells, zmaps, dens, shaded, sends,
+    row_send, row_got, near_send, near_got, far_send, far_got,
+    small_sem, brick_sem, live_sem, send_sem, box_sem,
+    row_sems, row_box, near_sems, near_box, far_sems, far_box,
 ):
     me = lax.axis_index("depth")
     tile = lax.axis_index("tile")
     my_x, my_y = tile // y_count, tile % y_count
+    near = sorted({hop % y_count for hop in (1, 2, -1, -2)} - {0})
+    far = sorted({hop % y_count for hop in (2, -2)} - {0})
 
     fetch_small = [
         pltpu.make_async_copy(there, here, small_sem.at[i])
@@ -98,7 +113,7 @@
         return carry
 
     lax.fori_loop(1, depth_count, greet_depth, 0)
-    for hop in range(1, y_count):
+    for hop in near:
         there = my_x * y_count + lax.rem(my_y + hop, y_count)
         pl.semaphore_signal(barrier, inc=1, device_id={"tile": there}, device_id_type=MESH)
     for hop in range(1, x_count):
@@ -147,22 +162,25 @@
     slopes = [slope[k] * 0.5 for k in range(3)]
     copies = []
 
-    def share_columns():
-        column = lax.broadcasted_iota(I32, (16, 128), 0)
-        values = jnp.zeros((16, 128), I32)
-        for b in range(16):
-            values = jnp.where(column == b, levels[0, b], values)
-        col_send[...] = values
-        col_got[my_y] = values
-        for hop in range(1, y_count):
-            there = my_x * y_count + lax.rem(my_y + hop, y_count)
+    def tell(source, target, hops, along_x, sends_sem, gets_sem):
+        for i, hop in enumerate(hops):
+            if along_x:
+                there = lax.rem(my_x + hop, x_count) * y_count + my_y
+            else:
+                there = my_x * y_count + lax.rem(my_y + hop, y_count)
             copy = pltpu.make_async_remote_copy(
-                src_ref=col_send, dst_ref=col_got.at[my_y],
-                send_sem=col_sems.at[hop], recv_sem=col_box.at[my_y],
+                src_ref=source, dst_ref=target.at[i],
+                send_sem=sends_sem.at[i], recv_sem=gets_sem.at[i],
                 device_id={"tile": there}, device_id_type=MESH,
             )
             copy.start()
             copies.append(copy)
+
+    def hear(target, hops, gets_sem):
+        for i in range(len(hops)):
+            pltpu.make_async_copy(target.at[i], target.at[i], gets_sem.at[i]).wait()
+
+    place = lax.broadcasted_iota(I32, (16, 128), 1)
 
     for half in range(2):
         gain = jnp.zeros((8, 128), F32)
@@ -186,42 +204,38 @@
                 through = after
                 for k in range(3):
                     sums[k] = sums[k] + glow * jnp.tanh(x * slopes[k])
-            solid = 1.0 - through
-            for k in range(3):
-                shaded[k, j] = 0.5 * (solid + sums[k])
-            shaded[3, j] = through
+            shaded[0, j], shaded[1, j] = encode(tau, 1.0 - through, sums)
             return carry
 
         lax.fori_loop(0, 8, shade, 0)
 
         source = (lane % 8) * 16 + (lane // 8 % 8) * 2 + lane // 64
         own_side = (lane // 64) == (sub // 4)
-        for pair in range(2):
-            sorted_lanes = []
-            for k in (2 * pair, 2 * pair + 1):
-                parts = [
-                    jnp.take_along_axis(shaded[k, j], source, axis=1, mode="promise_in_bounds")
-                    for j in range(8)
-                ]
-                for bit in range(3):
-                    step = 1 << bit
-                    upper = (lane // (8 * step)) % 2 == 1
-                    for j in range(8):
-                        if j & step:
-                            continue
-                        a, b = parts[j], parts[j + step]
-                        parts[j] = jnp.where(upper, pltpu.roll(b, 8 * step, 1), a)
-                        parts[j + step] = jnp.where(upper, b, pltpu.roll(a, 128 - 8 * step, 1))
-                sorted_lanes.append(
-                    [jnp.where(own_side, v, pltpu.roll(pltpu.roll(v, 64, 1), 4, 0)) for v in parts]
-                )
-            for g in range(8):
-                first, second = sorted_lanes[0][g], sorted_lanes[1][g]
-                sends[half, 2 * g, pair] = jnp.where(sub < 4, first, pltpu.roll(second, 4, 0))
-                sends[half, 2 * g + 1, pair] = jnp.where(sub < 4, pltpu.roll(first, 4, 0), second)
+        sorted_lanes = []
+        for k in range(2):
+            parts = [
+                jnp.take_along_axis(shaded[k, j], source, axis=1, mode="promise_in_bounds")
+                for j in range(8)
+            ]
+            for bit in range(3):
+                step = 1 << bit
+                upper = (lane // (8 * step)) % 2 == 1
+                for j in range(8):
+                    if j & step:
+                        continue
+                    a, b = parts[j], parts[j + step]
+                    parts[j] = jnp.where(upper, pltpu.roll(b, 8 * step, 1), a)
+                    parts[j + step] = jnp.where(upper, b, pltpu.roll(a, 128 - 8 * step, 1))
+            sorted_lanes.append(
+                [jnp.where(own_side, v, pltpu.roll(pltpu.roll(v, 64, 1), 4, 0)) for v in parts]
+            )
+        for g in range(8):
+            first, second = sorted_lanes[0][g], sorted_lanes[1][g]
+            sends[half, 2 * g] = jnp.where(sub < 4, first, pltpu.roll(second, 4, 0))
+            sends[half, 2 * g + 1] = jnp.where(sub < 4, pltpu.roll(first, 4, 0), second)
 
         if half == 0:
-            pl.semaphore_wait(barrier, depth_count - 1 + y_count - 1 + x_count - 1)
+            pl.semaphore_wait(barrier, depth_count - 1 + len(near) + x_count - 1)
         for hop in (8, 7, 9, 6, 10, 5, 11, 4, 12, 3, 13, 2, 14, 1, 15):
             to = lax.rem(me + hop, depth_count)
             copy = pltpu.make_async_remote_copy(
@@ -233,57 +247,68 @@
             copies.append(copy)
         boxes[half, me] = sends[half, me]
         if half == 0:
-            share_columns()
-
-    lane16 = lax.broadcasted_iota(I32, (16, 128), 1)
-    for hop in range(1, y_count):
-        there = lax.rem(my_y + hop, y_count)
-        pltpu.make_async_copy(col_got.at[there], col_got.at[there], col_box.at[there]).wait()
-    block = jnp.zeros((16, 128), I32)
-    for y in range(y_count):
-        block = jnp.where(lane16 % y_count == y, col_got[y], block)
-    block_send[...] = block
-    block_got[my_x] = block
+            column = lax.broadcasted_iota(I32, (16, 128), 0)
+            table = jnp.zeros((16, 128), I32)
+            for b in range(16):
+                table = jnp.where(column == b, levels[0, b], table)
+            row_send[...] = table
+            tell(row_send, row_got, range(1, x_count), True, row_sems, row_box)
+
+    hear(row_got, range(1, x_count), row_box)
     for hop in range(1, x_count):
-        there = lax.rem(my_x + hop, x_count) * y_count + my_y
-        copy = pltpu.make_async_remote_copy(
-            src_ref=block_send, dst_ref=block_got.at[my_x],
-            send_sem=block_sems.at[hop], recv_sem=block_box.at[my_x],
-            device_id={"tile": there}, device_id_type=MESH,
-        )
-        copy.start()
-        copies.append(copy)
-    for hop in range(1, x_count):
-        there = lax.rem(my_x + hop, x_count)
-        pltpu.make_async_copy(block_got.at[there], block_got.at[there], block_box.at[there]).wait()
-    grade = jnp.zeros((16, 128), I32)
-    for x in range(x_count):
-        grade = jnp.where(lane16 // y_count == x, block_got[x], grade)
-    grade = grade[:, 0 : x_count * y_count]
+        at = lax.rem(my_x + x_count - hop, x_count)
+        table = jnp.where(place // y_count == at, row_got[hop - 1], table)
+    near_send[...] = table
+    tell(near_send, near_got, near, False, near_sems, near_box)
+    hear(near_got, near, near_box)
+    for i, hop in enumerate(near):
+        at = lax.rem(my_y + y_count - hop, y_count)
+        table = jnp.where(place % y_count == at, near_got[i], table)
+    far_send[...] = table
+    tell(far_send, far_got, far, False, far_sems, far_box)
+    hear(far_got, far, far_box)
+    known = sorted({(-hop) % y_count for hop in near} | {0})
+    for i, hop in enumerate(far):
+        for step in sorted({(k - hop) % y_count for k in known} - set(known)):
+            at = lax.rem(my_y + step, y_count)
+            table = jnp.where(place % y_count == at, far_got[i], table)
+    grade = table[:, 0 : x_count * y_count]
     worth = jnp.where(grade == 2, 1.0, jnp.where(grade == 1, 0.25, 0.0625))
     share[...] = jnp.sum(jnp.where(owners[...] == tile, worth, 0.0), keepdims=True) * (1.0 / 16.0)
 
-    through = []
-    colors = []
     for half in range(2):
         for hop in range(1, depth_count):
             frm = lax.rem(me + hop, depth_count)
             pltpu.make_async_copy(boxes.at[half, frm], boxes.at[half, frm], box_sem.at[half, frm]).wait()
-        ahead = jnp.ones((8, 128), F32)
-        sums = [jnp.zeros((8, 128), F32)] * 2
-        for d in range(depth_count):
-            first, second = boxes[half, d, 0], boxes[half, d, 1]
-            sums = [sums[0] + ahead * first, sums[1] + ahead * second]
-            ahead = ahead * jnp.where(sub < 4, pltpu.roll(second, 4, 0), second)
-        through.append(ahead)
-        colors.append(sums)
-    low = sub < 4
-    out[0] = jnp.where(low, colors[0][0], pltpu.roll(colors[1][0], 4, 0))
-    out[1] = jnp.where(low, pltpu.roll(colors[0][0], 4, 0), colors[1][0])
-    out[2] = jnp.where(low, colors[0][1], pltpu.roll(colors[1][1], 4, 0))
-    out[3] = 1.0 - jnp.where(low, through[0], through[1])
     for copy in copies:
         copy.wait_send()
+
+
+def composite_kernel(depth_count, boxes, share_in, out, share):
+    low = lax.broadcasted_iota(I32, (8, 128), 0) < 4
+    passed, even, odd = [], [], []
+    for half in range(2):
+        ahead = jnp.ones((8, 128), F32)
+        first = jnp.zeros((8, 128), F32)
+        second = jnp.zeros((8, 128), F32)
+        for d in range(depth_count):
+            word = boxes[half, d]
+            bottom = (word & 65535).astype(F32)
+            top = lax.shift_right_logical(word, 16).astype(F32)
+            code = jnp.where(low, pltpu.roll(top, 4, 0), top)
+            through = jnp.exp(-jnp.exp2(code * (1.0 / CODE_SCALE) + CODE_FLOOR))
+            weight = ahead * (1.0 - through)
+            first = first + weight * bottom
+            second = second + weight * top
+            ahead = ahead * through
+        passed.append(ahead)
+        even.append(first * (1.0 / 65535.0))
+        odd.append(second * (1.0 / 65535.0))
+    out[0] = jnp.where(low, even[0], pltpu.roll(even[1], 4, 0))
+    out[1] = jnp.where(low, odd[0], pltpu.roll(odd[1], 4, 0))
+    out[2] = jnp.where(low, pltpu.roll(even[0], 4, 0), even[1])
+    out[3] = 1.0 - jnp.where(low, passed[0], passed[1])
+    share[...] = share_in[...]
 
 
 def local(bricks, levels, counts, gains, ownership, tf_slope):
@@ -292,13 +317,13 @@
     y_count = min(8, tile_count)
     x_count = tile_count // y_count
     vmem = pl.BlockSpec(memory_space=pltpu.VMEM)
-    anywhere = pl.BlockSpec(memory_space=pl.ANY)
+    anywhere = pl.BlockSpec(memory_space=pltpu.HBM)
     dma = pltpu.SemaphoreType.DMA
-    composite, share = pl.pallas_call(
+    boxes, share = pl.pallas_call(
         functools.partial(kernel, depth_count, x_count, y_count),
         out_shape=(
-            jax.ShapeDtypeStruct((4, 8, 128), F32),
-            jax.ShapeDtypeStruct((1, 1), F32),
+            pltpu.VMEM((2, 16, 8, 128), I32),
+            pltpu.VMEM((1, 1), F32),
         ),
         in_specs=[anywhere] * 6,
         out_specs=(vmem, vmem),
@@ -314,28 +339,42 @@
             pltpu.VMEM((512, 1024), BF16),
             pltpu.VMEM((2, 256, 256), BF16),
             pltpu.VMEM((2, 256, 1024), F32),
-            pltpu.VMEM((4, 8, 8, 128), F32),
-            pltpu.VMEM((2, 16, 2, 8, 128), F32),
-            pltpu.VMEM((2, 16, 2, 8, 128), F32),
+            pltpu.VMEM((2, 8, 8, 128), I32),
+            pltpu.VMEM((2, 16, 8, 128), I32),
             pltpu.VMEM((16, 128), I32),
-            pltpu.VMEM((8, 16, 128), I32),
+            pltpu.VMEM((3, 16, 128), I32),
             pltpu.VMEM((16, 128), I32),
             pltpu.VMEM((4, 16, 128), I32),
+            pltpu.VMEM((16, 128), I32),
+            pltpu.VMEM((2, 16, 128), I32),
             dma((4,)),
             dma((4,)),
             dma((8,)),
             dma((2, 16)),
             dma((2, 16)),
-            dma((8,)),
-            dma((8,)),
+            dma((3,)),
+            dma((3,)),
             dma((4,)),
             dma((4,)),
+            dma((2,)),
+            dma((2,)),
         ],
         compiler_params=pltpu.CompilerParams(
-            collective_id=0, has_side_effects=True, vmem_limit_bytes=60 * 1024 * 1024
+            collective_id=0, has_side_effects=True, vmem_limit_bytes=56000 * 1024
         ),
         name="render",
     )(bricks, levels, counts, gains, jnp.swapaxes(ownership, 1, 2), tf_slope)
+    composite, share = pl.pallas_call(
+        functools.partial(composite_kernel, depth_count),
+        out_shape=(
+            jax.ShapeDtypeStruct((4, 8, 128), F32),
+            jax.ShapeDtypeStruct((1, 1), F32),
+        ),
+        in_specs=[vmem, vmem],
+        out_specs=(vmem, vmem),
+        compiler_params=pltpu.CompilerParams(vmem_limit_bytes=4 * 1024 * 1024),
+        name="composite",
+    )(boxes, share)
     return composite.reshape(4, 1, 1024), share
 
 

time: 28.4 us -> 27.4 us (0.965)
  Pallas kernels: 24.4 us -> 26.4 us
  between operations: 2.4 us -> 0.64 us
  local copies, waits for them, and re-layouts: 1.32 us -> 0 us
    pallas_call x0 -> x1, Pallas kernels: none -> 1.33 us  [local(): pl.pallas_call(functools.partial(composite_kernel, depth_count), out_shap...]
    unnamed x1 -> x0, local copies, waits for them, and re-layouts: 1.32 us -> none
    pallas_call x1, Pallas kernels: 24.4 us -> 25.1 us  [local(): pl.pallas_call(functools.partial(kernel, depth_count, x_count, y_count),...]
where the time goes in v3:
time: 27.4 us; the launch traced here: 27 us
  Pallas kernels  26.4 us (96%)
  between operations  0.64 us (2%)
    pallas_call x1, Pallas kernels, local(): pl.pallas_call(functools.partial(kernel, depth_count, x_count, y_count),...  25.1 us
    pallas_call x1, Pallas kernels, local(): pl.pallas_call(functools.partial(composite_kernel, depth_count), out_shap...  1.33 us

profile of v3, /device:TPU:1, one launch (start us, length us, event | category | flops | bytes accessed | tf_op | source)
XLA Modules:
  0.0 27.0 jit_solution(15124639296317885713)
XLA Ops:
  0.6 25.1 %render.1 = (s32[2,16,8,128]{3,2,1,0:T(8,128)S(1)}, f32[1,1]{1,0:T(1,128)}) custom-call(bf16[1,16,32,1024]{3,2,1,0:T(8,128)(2,1)} %bricks.1, s32[1,16]{1,0:T(1,128)} %levels_in.1, s32[1,16,1024]{2,1,0:T(8,128)} %counts.1, f32[1,16]{1,0:T(1,128)} %gains_in.1, s32[1,16,32]{2,1,0:T(8,128)} %bitcast.2, f32[3]{0:T(128)} %slope_in.1), custom_call_target="tpu_custom_call" | custom-call | tf_op jit(solution)/shard_map/render/pallas_call | solution.py:322
  25.7 1.3 %composite.1 = (f32[4,8,128]{2,1,0:T(8,128)}, f32[1,1]{1,0:T(1,128)}) custom-call(s32[2,16,8,128]{3,2,1,0:T(8,128)S(1)} %get-tuple-element.6.boxes, f32[1,1]{1,0:T(1,128)} %get-tuple-element.7.share_in), custom_call_target="tpu_custom_call" | custom-call | tf_op jit(solution)/shard_map/composite/pallas_call | solution.py:367

commit v4 on v3

--- a/solution.py
+++ b/solution.py
@@ -73,21 +73,39 @@
     return codes[0] | (codes[1] << 16), codes[2] | (codes[3] << 16)
 
 
+def swapped(place):
+    return place + 1 - 2 * (place % 2)
+
+
+def wait_for(semaphore, count):
+    @pl.when(count > 0)
+    def _():
+        pl.semaphore_wait(semaphore, count)
+
+
+def y_order(y, count):
+    back = count - y
+    return jnp.where(y <= back, jnp.maximum(2 * y - 1, 0), 2 * back)
+
+
+def y_at(order, count):
+    return jnp.where(order % 2 == 1, (order + 1) // 2, (count - order // 2) % count)
+
+
 def kernel(
     depth_count, x_count, y_count,
     bricks, levels_in, counts, gains_in, owners_in, slope_in,
     boxes, share,
     levels, gains, slope, owners,
     raw, lives, masked, maps, cells, zmaps, dens, shaded, sends,
-    row_send, row_got, near_send, near_got, far_send, far_got,
+    row_send, block_send, x_rows, y_rows,
     small_sem, brick_sem, live_sem, send_sem, box_sem,
-    row_sems, row_box, near_sems, near_box, far_sems, far_box,
+    row_sem, row_box, depth_ready, x_ready, y_ready,
 ):
     me = lax.axis_index("depth")
     tile = lax.axis_index("tile")
+    tile_count = x_count * y_count
     my_x, my_y = tile // y_count, tile % y_count
-    near = sorted({hop % y_count for hop in (1, 2, -1, -2)} - {0})
-    far = sorted({hop % y_count for hop in (2, -2)} - {0})
 
     fetch_small = [
         pltpu.make_async_copy(there, here, small_sem.at[i])
@@ -103,22 +121,34 @@
         pltpu.make_async_copy(counts.at[0, :, pl.ds(j * 128, 128)], lives.at[j], live_sem.at[j])
         for j in range(8)
     ]
-    for copy in fetch_small + fetch_bricks + fetch_lives:
+    for copy in fetch_bricks + fetch_small + fetch_lives:
         copy.start()
 
     barrier = pltpu.get_barrier_semaphore()
-
-    def greet_depth(hop, carry):
-        pl.semaphore_signal(barrier, inc=1, device_id={"depth": lax.rem(me + hop, depth_count)}, device_id_type=MESH)
+    order = swapped(me)
+
+    def greet(peer, carry):
+        pl.semaphore_signal(barrier, inc=1, device_id={"depth": swapped(peer)}, device_id_type=MESH)
         return carry
 
-    lax.fori_loop(1, depth_count, greet_depth, 0)
-    for hop in near:
-        there = my_x * y_count + lax.rem(my_y + hop, y_count)
-        pl.semaphore_signal(barrier, inc=1, device_id={"tile": there}, device_id_type=MESH)
-    for hop in range(1, x_count):
-        there = lax.rem(my_x + hop, x_count) * y_count + my_y
-        pl.semaphore_signal(barrier, inc=1, device_id={"tile": there}, device_id_type=MESH)
+    lax.fori_loop(order + 1, depth_count, greet, 0)
+    my_order = y_order(my_y, y_count)
+
+    def at_x(x):
+        return {"tile": x * y_count + my_y}
+
+    def at_y(place):
+        return {"tile": my_x * y_count + y_at(place, y_count)}
+
+    def signal(semaphore, device):
+        def one(peer, carry):
+            pl.semaphore_signal(semaphore, inc=1, device_id=device(peer), device_id_type=MESH)
+            return carry
+
+        return one
+
+    lax.fori_loop(my_x + 1, x_count, signal(barrier, at_x), 0)
+    lax.fori_loop(my_order + 1, y_count, signal(barrier, at_y), 0)
 
     fill_plane_maps(maps)
     for copy in fetch_small:
@@ -160,27 +190,47 @@
     for copy in fetch_lives:
         copy.wait()
     slopes = [slope[k] * 0.5 for k in range(3)]
-    copies = []
-
-    def tell(source, target, hops, along_x, sends_sem, gets_sem):
-        for i, hop in enumerate(hops):
-            if along_x:
-                there = lax.rem(my_x + hop, x_count) * y_count + my_y
-            else:
-                there = my_x * y_count + lax.rem(my_y + hop, y_count)
-            copy = pltpu.make_async_remote_copy(
-                src_ref=source, dst_ref=target.at[i],
-                send_sem=sends_sem.at[i], recv_sem=gets_sem.at[i],
-                device_id={"tile": there}, device_id_type=MESH,
-            )
-            copy.start()
-            copies.append(copy)
-
-    def hear(target, hops, gets_sem):
-        for i in range(len(hops)):
-            pltpu.make_async_copy(target.at[i], target.at[i], gets_sem.at[i]).wait()
-
-    place = lax.broadcasted_iota(I32, (16, 128), 1)
+
+    def pixels(half, to):
+        return pltpu.make_async_remote_copy(
+            src_ref=sends.at[half, to], dst_ref=boxes.at[half, me],
+            send_sem=send_sem.at[half], recv_sem=box_sem.at[half],
+            device_id={"depth": to}, device_id_type=MESH,
+        )
+
+    def send(half, peer, carry):
+        pixels(half, swapped(peer)).start()
+        return carry
+
+    def along_x(x):
+        return pltpu.make_async_remote_copy(
+            src_ref=row_send, dst_ref=x_rows.at[my_x], send_sem=row_sem.at[0], recv_sem=row_box.at[0],
+            device_id=at_x(x), device_id_type=MESH,
+        )
+
+    def along_y(place):
+        return pltpu.make_async_remote_copy(
+            src_ref=block_send, dst_ref=y_rows.at[my_y], send_sem=row_sem.at[1], recv_sem=row_box.at[1],
+            device_id=at_y(place), device_id_type=MESH,
+        )
+
+    def start(copy):
+        def one(peer, carry):
+            copy(peer).start()
+            return carry
+
+        return one
+
+    def take(buffer, count, semaphore):
+        if count:
+            some = buffer.at[pl.ds(0, count)]
+            pltpu.make_async_copy(some, some, semaphore).wait()
+
+    packed = jnp.zeros((8, 128), I32)
+    for s in range(8):
+        packed = jnp.where(sub == s, levels[0, s] + 256 * levels[0, s + 8], packed)
+    row_send[...] = packed
+    x_rows[my_x] = packed
 
     for half in range(2):
         gain = jnp.zeros((8, 128), F32)
@@ -235,53 +285,50 @@
             sends[half, 2 * g + 1] = jnp.where(sub < 4, pltpu.roll(first, 4, 0), second)
 
         if half == 0:
-            pl.semaphore_wait(barrier, depth_count - 1 + len(near) + x_count - 1)
-        for hop in (8, 7, 9, 6, 10, 5, 11, 4, 12, 3, 13, 2, 14, 1, 15):
-            to = lax.rem(me + hop, depth_count)
-            copy = pltpu.make_async_remote_copy(
-                src_ref=sends.at[half, to], dst_ref=boxes.at[half, me],
-                send_sem=send_sem.at[half, hop], recv_sem=box_sem.at[half, me],
-                device_id={"depth": to}, device_id_type=MESH,
-            )
-            copy.start()
-            copies.append(copy)
+            wait_for(barrier, order + my_x + my_order)
+        lax.fori_loop(0, order, functools.partial(send, half), 0)
         boxes[half, me] = sends[half, me]
-        if half == 0:
-            column = lax.broadcasted_iota(I32, (16, 128), 0)
-            table = jnp.zeros((16, 128), I32)
-            for b in range(16):
-                table = jnp.where(column == b, levels[0, b], table)
-            row_send[...] = table
-            tell(row_send, row_got, range(1, x_count), True, row_sems, row_box)
-
-    hear(row_got, range(1, x_count), row_box)
-    for hop in range(1, x_count):
-        at = lax.rem(my_x + x_count - hop, x_count)
-        table = jnp.where(place // y_count == at, row_got[hop - 1], table)
-    near_send[...] = table
-    tell(near_send, near_got, near, False, near_sems, near_box)
-    hear(near_got, near, near_box)
-    for i, hop in enumerate(near):
-        at = lax.rem(my_y + y_count - hop, y_count)
-        table = jnp.where(place % y_count == at, near_got[i], table)
-    far_send[...] = table
-    tell(far_send, far_got, far, False, far_sems, far_box)
-    hear(far_got, far, far_box)
-    known = sorted({(-hop) % y_count for hop in near} | {0})
-    for i, hop in enumerate(far):
-        for step in sorted({(k - hop) % y_count for k in known} - set(known)):
-            at = lax.rem(my_y + step, y_count)
-            table = jnp.where(place % y_count == at, far_got[i], table)
-    grade = table[:, 0 : x_count * y_count]
-    worth = jnp.where(grade == 2, 1.0, jnp.where(grade == 1, 0.25, 0.0625))
-    share[...] = jnp.sum(jnp.where(owners[...] == tile, worth, 0.0), keepdims=True) * (1.0 / 16.0)
-
-    for half in range(2):
-        for hop in range(1, depth_count):
-            frm = lax.rem(me + hop, depth_count)
-            pltpu.make_async_copy(boxes.at[half, frm], boxes.at[half, frm], box_sem.at[half, frm]).wait()
-    for copy in copies:
-        copy.wait_send()
+    lax.fori_loop(0, order, signal(depth_ready, lambda peer: {"depth": swapped(peer)}), 0)
+    lax.fori_loop(0, my_x, signal(x_ready, at_x), 0)
+    lax.fori_loop(0, my_order, signal(y_ready, at_y), 0)
+    lax.fori_loop(0, my_x, start(along_x), 0)
+
+    def serve_later():
+        wait_for(depth_ready, depth_count - 1 - order)
+        for half in range(2):
+            lax.fori_loop(order + 1, depth_count, functools.partial(send, half), 0)
+
+    pl.when(me >= depth_count // 2)(serve_later)
+
+    wait_for(x_ready, x_count - 1 - my_x)
+    lax.fori_loop(my_x + 1, x_count, start(along_x), 0)
+    take(x_rows, x_count - 1, row_box.at[0])
+    table = jnp.zeros((8, 128), I32)
+    for x in range(x_count):
+        table = jnp.where(lane // y_count == x, x_rows[x], table)
+    block_send[...] = table
+    y_rows[my_y] = table
+    wait_for(y_ready, y_count - 1 - my_order)
+    lax.fori_loop(0, my_order, start(along_y), 0)
+    lax.fori_loop(my_order + 1, y_count, start(along_y), 0)
+    take(y_rows, y_count - 1, row_box.at[1])
+    for y in range(y_count):
+        table = jnp.where(lane % y_count == y, y_rows[y], table)
+    table = table[:, 0:tile_count]
+    total = jnp.zeros((8, tile_count), F32)
+    for part, grade in enumerate((table & 255, table >> 8)):
+        worth = jnp.where(grade == 2, 1.0, jnp.where(grade == 1, 0.25, 0.0625))
+        total = total + jnp.where(owners[8 * part : 8 * part + 8] == tile, worth, 0.0)
+    share[...] = jnp.sum(total, keepdims=True) * (1.0 / 16.0)
+
+    pl.when(me < depth_count // 2)(serve_later)
+
+    take(x_rows, x_count - 1, row_sem.at[0])
+    take(y_rows, y_count - 1, row_sem.at[1])
+    for half in range(2):
+        take(sends.at[half], depth_count - 1, send_sem.at[half])
+    for half in range(2):
+        take(boxes.at[half], depth_count - 1, box_sem.at[half])
 
 
 def composite_kernel(depth_count, boxes, share_in, out, share):
@@ -341,23 +388,20 @@
             pltpu.VMEM((2, 256, 1024), F32),
             pltpu.VMEM((2, 8, 8, 128), I32),
             pltpu.VMEM((2, 16, 8, 128), I32),
-            pltpu.VMEM((16, 128), I32),
-            pltpu.VMEM((3, 16, 128), I32),
-            pltpu.VMEM((16, 128), I32),
-            pltpu.VMEM((4, 16, 128), I32),
-            pltpu.VMEM((16, 128), I32),
-            pltpu.VMEM((2, 16, 128), I32),
+            pltpu.VMEM((8, 128), I32),
+            pltpu.VMEM((8, 128), I32),
+            pltpu.VMEM((x_count, 8, 128), I32),
+            pltpu.VMEM((y_count, 8, 128), I32),
             dma((4,)),
             dma((4,)),
             dma((8,)),
-            dma((2, 16)),
-            dma((2, 16)),
-            dma((3,)),
-            dma((3,)),
-            dma((4,)),
-            dma((4,)),
             dma((2,)),
             dma((2,)),
+            dma((2,)),
+            dma((2,)),
+            pltpu.SemaphoreType.REGULAR,
+            pltpu.SemaphoreType.REGULAR,
+            pltpu.SemaphoreType.REGULAR,
         ],
         compiler_params=pltpu.CompilerParams(
             collective_id=0, has_side_effects=True, vmem_limit_bytes=56000 * 1024

time: 27.4 us -> 23.8 us (0.87)
  the two profiles are of different devices: /device:TPU:1 before, /device:TPU:132 now
where the time goes in v4:
time: 23.8 us; the launch traced here: 23.6 us
  Pallas kernels  23 us (97%)
  between operations  0.64 us (3%)
    pallas_call x1, Pallas kernels, local(): pl.pallas_call(functools.partial(kernel, depth_count, x_count, y_count),...  21.6 us
    pallas_call x1, Pallas kernels, local(): pl.pallas_call(functools.partial(composite_kernel, depth_count), out_shap...  1.33 us

profile of v4, /device:TPU:132, one launch (start us, length us, event | category | flops | bytes accessed | tf_op | source)
XLA Modules:
  0.0 23.6 jit_solution(12767009564339768373)
XLA Ops:
  0.6 21.6 %render.1 = (s32[2,16,8,128]{3,2,1,0:T(8,128)S(1)}, f32[1,1]{1,0:T(1,128)}) custom-call(bf16[1,16,32,1024]{3,2,1,0:T(8,128)(2,1)} %bricks.1, s32[1,16]{1,0:T(1,128)} %levels_in.1, s32[1,16,1024]{2,1,0:T(8,128)} %counts.1, f32[1,16]{1,0:T(1,128)} %gains_in.1, s32[1,16,32]{2,1,0:T(8,128)} %bitcast.2, f32[3]{0:T(128)} %slope_in.1), custom_call_target="tpu_custom_call" | custom-call | tf_op jit(solution)/shard_map/render/pallas_call | solution.py:369
  22.3 1.3 %composite.1 = (f32[4,8,128]{2,1,0:T(8,128)}, f32[1,1]{1,0:T(1,128)}) custom-call(s32[2,16,8,128]{3,2,1,0:T(8,128)S(1)} %get-tuple-element.6.boxes, f32[1,1]{1,0:T(1,128)} %get-tuple-element.7.share_in), custom_call_target="tpu_custom_call" | custom-call | tf_op jit(solution)/shard_map/composite/pallas_call | solution.py:411

commit v5 on v4

--- a/solution.py
+++ b/solution.py
@@ -231,6 +231,8 @@
         packed = jnp.where(sub == s, levels[0, s] + 256 * levels[0, s + 8], packed)
     row_send[...] = packed
     x_rows[my_x] = packed
+
+    source = (lane % 8) * 16 + (lane // 8 % 8) * 2 + lane // 64
 
     for half in range(2):
         gain = jnp.zeros((8, 128), F32)
@@ -259,14 +261,16 @@
 
         lax.fori_loop(0, 8, shade, 0)
 
-        source = (lane % 8) * 16 + (lane // 8 % 8) * 2 + lane // 64
-        own_side = (lane // 64) == (sub // 4)
-        sorted_lanes = []
-        for k in range(2):
-            parts = [
-                jnp.take_along_axis(shaded[k, j], source, axis=1, mode="promise_in_bounds")
-                for j in range(8)
-            ]
+        kinds = []
+        for kind in range(2):
+            parts = []
+            for j in range(8):
+                first, second = shaded[0, j], shaded[1, j]
+                if kind == 0:
+                    words = jnp.where(sub < 4, first, pltpu.roll(second, 4, 0))
+                else:
+                    words = jnp.where(sub < 4, pltpu.roll(first, 4, 0), second)
+                parts.append(jnp.take_along_axis(words, source, axis=1, mode="promise_in_bounds"))
             for bit in range(3):
                 step = 1 << bit
                 upper = (lane // (8 * step)) % 2 == 1
@@ -276,32 +280,29 @@
                     a, b = parts[j], parts[j + step]
                     parts[j] = jnp.where(upper, pltpu.roll(b, 8 * step, 1), a)
                     parts[j + step] = jnp.where(upper, b, pltpu.roll(a, 128 - 8 * step, 1))
-            sorted_lanes.append(
-                [jnp.where(own_side, v, pltpu.roll(pltpu.roll(v, 64, 1), 4, 0)) for v in parts]
-            )
+            kinds.append(parts)
         for g in range(8):
-            first, second = sorted_lanes[0][g], sorted_lanes[1][g]
-            sends[half, 2 * g] = jnp.where(sub < 4, first, pltpu.roll(second, 4, 0))
-            sends[half, 2 * g + 1] = jnp.where(sub < 4, pltpu.roll(first, 4, 0), second)
+            even, odd = kinds[0][g], kinds[1][g]
+            sends[half, 2 * g] = jnp.where(lane < 64, even, pltpu.roll(odd, 64, 1))
+            sends[half, 2 * g + 1] = jnp.where(lane < 64, pltpu.roll(even, 64, 1), odd)
 
         if half == 0:
             wait_for(barrier, order + my_x + my_order)
+            lax.fori_loop(0, my_x, signal(x_ready, at_x), 0)
+            lax.fori_loop(0, my_x, start(along_x), 0)
+            lax.fori_loop(0, my_order, signal(y_ready, at_y), 0)
         lax.fori_loop(0, order, functools.partial(send, half), 0)
         boxes[half, me] = sends[half, me]
     lax.fori_loop(0, order, signal(depth_ready, lambda peer: {"depth": swapped(peer)}), 0)
-    lax.fori_loop(0, my_x, signal(x_ready, at_x), 0)
-    lax.fori_loop(0, my_order, signal(y_ready, at_y), 0)
-    lax.fori_loop(0, my_x, start(along_x), 0)
 
     def serve_later():
         wait_for(depth_ready, depth_count - 1 - order)
         for half in range(2):
             lax.fori_loop(order + 1, depth_count, functools.partial(send, half), 0)
 
-    pl.when(me >= depth_count // 2)(serve_later)
-
     wait_for(x_ready, x_count - 1 - my_x)
     lax.fori_loop(my_x + 1, x_count, start(along_x), 0)
+    pl.when(me >= depth_count // 2)(serve_later)
     take(x_rows, x_count - 1, row_box.at[0])
     table = jnp.zeros((8, 128), I32)
     for x in range(x_count):

time: 23.8 us -> 22.8 us (0.958)
  the two profiles are of different devices: /device:TPU:132 before, /device:TPU:2 now
where the time goes in v5:
time: 22.8 us; the launch traced here: 22.7 us
  Pallas kernels  22 us (96%)
  between operations  0.64 us (3%)
    pallas_call x1, Pallas kernels, local(): pl.pallas_call(functools.partial(kernel, depth_count, x_count, y_count),...  20.7 us
    pallas_call x1, Pallas kernels, local(): pl.pallas_call(functools.partial(composite_kernel, depth_count), out_shap...  1.33 us

profile of v5, /device:TPU:2, one launch (start us, length us, event | category | flops | bytes accessed | tf_op | source)
XLA Modules:
  0.0 22.7 jit_solution(11475943131626231727)
XLA Ops:
  0.6 20.7 %render.1 = (s32[2,16,8,128]{3,2,1,0:T(8,128)S(1)}, f32[1,1]{1,0:T(1,128)}) custom-call(bf16[1,16,32,1024]{3,2,1,0:T(8,128)(2,1)} %bricks.1, s32[1,16]{1,0:T(1,128)} %levels_in.1, s32[1,16,1024]{2,1,0:T(8,128)} %counts.1, f32[1,16]{1,0:T(1,128)} %gains_in.1, s32[1,16,32]{2,1,0:T(8,128)} %bitcast.2, f32[3]{0:T(128)} %slope_in.1), custom_call_target="tpu_custom_call" | custom-call | tf_op jit(solution)/shard_map/render/pallas_call | solution.py:370
  21.3 1.3 %composite.1 = (f32[4,8,128]{2,1,0:T(8,128)}, f32[1,1]{1,0:T(1,128)}) custom-call(s32[2,16,8,128]{3,2,1,0:T(8,128)S(1)} %get-tuple-element.6.boxes, f32[1,1]{1,0:T(1,128)} %get-tuple-element.7.share_in), custom_call_target="tpu_custom_call" | custom-call | tf_op jit(solution)/shard_map/composite/pallas_call | solution.py:412

commit v6 on v5

--- a/solution.py
+++ b/solution.py
@@ -293,7 +293,8 @@
             lax.fori_loop(0, my_order, signal(y_ready, at_y), 0)
         lax.fori_loop(0, order, functools.partial(send, half), 0)
         boxes[half, me] = sends[half, me]
-    lax.fori_loop(0, order, signal(depth_ready, lambda peer: {"depth": swapped(peer)}), 0)
+        if half == 0:
+            lax.fori_loop(0, order, signal(depth_ready, lambda peer: {"depth": swapped(peer)}), 0)
 
     def serve_later():
         wait_for(depth_ready, depth_count - 1 - order)
@@ -312,6 +313,7 @@
     wait_for(y_ready, y_count - 1 - my_order)
     lax.fori_loop(0, my_order, start(along_y), 0)
     lax.fori_loop(my_order + 1, y_count, start(along_y), 0)
+    pl.when(me < depth_count // 2)(serve_later)
     take(y_rows, y_count - 1, row_box.at[1])
     for y in range(y_count):
         table = jnp.where(lane % y_count == y, y_rows[y], table)
@@ -321,8 +323,6 @@
         worth = jnp.where(grade == 2, 1.0, jnp.where(grade == 1, 0.25, 0.0625))
         total = total + jnp.where(owners[8 * part : 8 * part + 8] == tile, worth, 0.0)
     share[...] = jnp.sum(total, keepdims=True) * (1.0 / 16.0)
-
-    pl.when(me < depth_count // 2)(serve_later)
 
     take(x_rows, x_count - 1, row_sem.at[0])
     take(y_rows, y_count - 1, row_sem.at[1])

time: 22.8 us -> 21.1 us (0.925)
  the two profiles are of different devices: /device:TPU:2 before, /device:TPU:1 now
where the time goes in v6:
time: 21.1 us; the launch traced here: 21 us
  Pallas kernels  20.3 us (96%)
  between operations  0.64 us (3%)
    pallas_call x1, Pallas kernels, local(): pl.pallas_call(functools.partial(kernel, depth_count, x_count, y_count),...  19 us
    pallas_call x1, Pallas kernels, local(): pl.pallas_call(functools.partial(composite_kernel, depth_count), out_shap...  1.33 us

profile of v6, /device:TPU:1, one launch (start us, length us, event | category | flops | bytes accessed | tf_op | source)
XLA Modules:
  0.0 21.0 jit_solution(6901705117952036585)
XLA Ops:
  0.6 19.0 %render.1 = (s32[2,16,8,128]{3,2,1,0:T(8,128)S(1)}, f32[1,1]{1,0:T(1,128)}) custom-call(bf16[1,16,32,1024]{3,2,1,0:T(8,128)(2,1)} %bricks.1, s32[1,16]{1,0:T(1,128)} %levels_in.1, s32[1,16,1024]{2,1,0:T(8,128)} %counts.1, f32[1,16]{1,0:T(1,128)} %gains_in.1, s32[1,16,32]{2,1,0:T(8,128)} %bitcast.2, f32[3]{0:T(128)} %slope_in.1), custom_call_target="tpu_custom_call" | custom-call | tf_op jit(solution)/shard_map/render/pallas_call | solution.py:370
  19.6 1.3 %composite.1 = (f32[4,8,128]{2,1,0:T(8,128)}, f32[1,1]{1,0:T(1,128)}) custom-call(s32[2,16,8,128]{3,2,1,0:T(8,128)S(1)} %get-tuple-element.6.boxes, f32[1,1]{1,0:T(1,128)} %get-tuple-element.7.share_in), custom_call_target="tpu_custom_call" | custom-call | tf_op jit(solution)/shard_map/composite/pallas_call | solution.py:412

commit v7 on v6

--- a/solution.py
+++ b/solution.py
@@ -95,10 +95,10 @@
 def kernel(
     depth_count, x_count, y_count,
     bricks, levels_in, counts, gains_in, owners_in, slope_in,
-    boxes, share,
+    out, share,
     levels, gains, slope, owners,
     raw, lives, masked, maps, cells, zmaps, dens, shaded, sends,
-    row_send, block_send, x_rows, y_rows,
+    row_send, block_send, x_rows, y_rows, boxes,
     small_sem, brick_sem, live_sem, send_sem, box_sem,
     row_sem, row_box, depth_ready, x_ready, y_ready,
 ):
@@ -239,14 +239,22 @@
         for s in range(8):
             gain = jnp.where(sub == s, -gains[0, brick_of(8 * half + s)], gain)
 
-        def shade(j, carry, half=half, gain=gain):
-            lanes = pl.ds(pl.multiple_of(j * 128, 128), 128)
+        gain = jnp.concatenate([gain, gain], axis=1)
+
+        def shade(n, carry, half=half, gain=gain):
+            lanes = pl.ds(pl.multiple_of(n * 256, 256), 256)
             live = jnp.concatenate(
-                [lives[j, pl.ds(8 * half + odd, 4, stride=2), :] for odd in range(2)], axis=0
+                [
+                    jnp.concatenate(
+                        [lives[2 * n + j, pl.ds(8 * half + odd, 4, stride=2), :] for odd in range(2)], axis=0
+                    )
+                    for j in range(2)
+                ],
+                axis=1,
             )
-            tau = jnp.zeros((8, 128), F32)
-            through = jnp.ones((8, 128), F32)
-            sums = [jnp.zeros((8, 128), F32)] * 3
+            tau = jnp.zeros((8, 256), F32)
+            through = jnp.ones((8, 256), F32)
+            sums = [jnp.zeros((8, 256), F32)] * 3
             for z in range(32):
                 x = dens[half, z * 8 : z * 8 + 8, lanes]
                 soft = jnp.log(1.0 + jnp.exp(x))
@@ -256,10 +264,12 @@
                 through = after
                 for k in range(3):
                     sums[k] = sums[k] + glow * jnp.tanh(x * slopes[k])
-            shaded[0, j], shaded[1, j] = encode(tau, 1.0 - through, sums)
+            for k, words in enumerate(encode(tau, 1.0 - through, sums)):
+                for j in range(2):
+                    shaded[k, 2 * n + j] = words[:, 128 * j : 128 * j + 128]
             return carry
 
-        lax.fori_loop(0, 8, shade, 0)
+        lax.fori_loop(0, 4, shade, 0)
 
         kinds = []
         for kind in range(2):
@@ -330,9 +340,6 @@
         take(sends.at[half], depth_count - 1, send_sem.at[half])
     for half in range(2):
         take(boxes.at[half], depth_count - 1, box_sem.at[half])
-
-
-def composite_kernel(depth_count, boxes, share_in, out, share):
     low = lax.broadcasted_iota(I32, (8, 128), 0) < 4
     passed, even, odd = [], [], []
     for half in range(2):
@@ -356,7 +363,6 @@
     out[1] = jnp.where(low, odd[0], pltpu.roll(odd[1], 4, 0))
     out[2] = jnp.where(low, pltpu.roll(even[0], 4, 0), even[1])
     out[3] = 1.0 - jnp.where(low, passed[0], passed[1])
-    share[...] = share_in[...]
 
 
 def local(bricks, levels, counts, gains, ownership, tf_slope):
@@ -367,10 +373,10 @@
     vmem = pl.BlockSpec(memory_space=pltpu.VMEM)
     anywhere = pl.BlockSpec(memory_space=pltpu.HBM)
     dma = pltpu.SemaphoreType.DMA
-    boxes, share = pl.pallas_call(
+    composite, share = pl.pallas_call(
         functools.partial(kernel, depth_count, x_count, y_count),
         out_shape=(
-            pltpu.VMEM((2, 16, 8, 128), I32),
+            pltpu.VMEM((4, 8, 128), F32),
             pltpu.VMEM((1, 1), F32),
         ),
         in_specs=[anywhere] * 6,
@@ -393,6 +399,7 @@
             pltpu.VMEM((8, 128), I32),
             pltpu.VMEM((x_count, 8, 128), I32),
             pltpu.VMEM((y_count, 8, 128), I32),
+            pltpu.VMEM((2, 16, 8, 128), I32),
             dma((4,)),
             dma((4,)),
             dma((8,)),
@@ -409,17 +416,6 @@
         ),
         name="render",
     )(bricks, levels, counts, gains, jnp.swapaxes(ownership, 1, 2), tf_slope)
-    composite, share = pl.pallas_call(
-        functools.partial(composite_kernel, depth_count),
-        out_shape=(
-            jax.ShapeDtypeStruct((4, 8, 128), F32),
-            jax.ShapeDtypeStruct((1, 1), F32),
-        ),
-        in_specs=[vmem, vmem],
-        out_specs=(vmem, vmem),
-        compiler_params=pltpu.CompilerParams(vmem_limit_bytes=4 * 1024 * 1024),
-        name="composite",
-    )(boxes, share)
     return composite.reshape(4, 1, 1024), share
 
 

time: 21.1 us -> 20.3 us (0.962)
  Pallas kernels: 20.3 us -> 18.4 us
  local copies, waits for them, and re-layouts: 0 us -> 0.6 us
  between operations: 0.64 us -> 1.18 us
    pallas_call x1 -> x0, Pallas kernels: 1.33 us -> none  [local(): pl.pallas_call(functools.partial(composite_kernel, depth_count), out_shap...]
    unnamed x0 -> x1, local copies, waits for them, and re-layouts: none -> 0.6 us
    pallas_call x1, Pallas kernels: 19 us -> 18.4 us  [local(): pl.pallas_call(functools.partial(kernel, depth_count, x_count, y_count),...]
where the time goes in v7:
time: 20.3 us; the launch traced here: 20.2 us
  Pallas kernels  18.4 us (91%)
  between operations  1.18 us (6%)
  local copies, waits for them, and re-layouts  0.6 us (3%)
    pallas_call x1, Pallas kernels, local(): pl.pallas_call(functools.partial(kernel, depth_count, x_count, y_count),...  18.4 us
    unnamed x1, local copies, waits for them, and re-layouts  0.6 us

profile of v7, /device:TPU:1, one launch (start us, length us, event | category | flops | bytes accessed | tf_op | source)
XLA Modules:
  0.0 20.2 jit_solution(7740071738696248620)
XLA Ops:
  0.6 18.4 %render.1 = (f32[4,8,128]{2,1,0:T(8,128)S(1)}, f32[1,1]{1,0:T(1,128)S(1)}) custom-call(bf16[1,16,32,1024]{3,2,1,0:T(8,128)(2,1)} %bricks.1, s32[1,16]{1,0:T(1,128)} %levels_in.1, s32[1,16,1024]{2,1,0:T(8,128)} %counts.1, f32[1,16]{1,0:T(1,128)} %gains_in.1, s32[1,16,32]{2,1,0:T(8,128)} %bitcast.3, f32[3]{0:T(128)} %slope_in.1), custom_call_target="tpu_custom_call" | custom-call | tf_op jit(solution)/shard_map/render/pallas_call | solution.py:376
  19.6 0.6 %copy.11 = f32[4,1,1024]{2,1,0:T(1,128)} copy(f32[4,1,1024]{2,1,0:T(1,128)S(1)} %bitcast.2) | data formatting | bytes 32768

commit v8 on v7

--- a/solution.py
+++ b/solution.py
@@ -12,6 +12,8 @@
 I32 = jnp.int32
 MESH = pl.DeviceIdType.MESH
 CODE_FLOOR = -20.75
+LOG2_E = 1.4426950408889634
+LN_2 = 0.6931471805599453
 CODE_SCALE = 65535.0 / 23.75
 
 
@@ -68,7 +70,7 @@
     codes = [
         jnp.clip(sums[k] * scale + 32768.0, 0.0, 65535.0).astype(I32) for k in range(3)
     ]
-    depth = jnp.log2(jnp.maximum(-tau, 1e-12))
+    depth = jnp.log2(jnp.maximum(tau * -LN_2, 1e-12))
     codes.append(jnp.clip((depth - CODE_FLOOR) * CODE_SCALE + 0.5, 0.0, 65535.0).astype(I32))
     return codes[0] | (codes[1] << 16), codes[2] | (codes[3] << 16)
 
@@ -257,9 +259,9 @@
             sums = [jnp.zeros((8, 256), F32)] * 3
             for z in range(32):
                 x = dens[half, z * 8 : z * 8 + 8, lanes]
-                soft = jnp.log(1.0 + jnp.exp(x))
+                soft = jnp.log2(1.0 + jnp.exp2(x * LOG2_E))
                 tau = tau + jnp.where(live > z, soft * gain, 0.0)
-                after = jnp.exp(tau)
+                after = jnp.exp2(tau)
                 glow = through - after
                 through = after
                 for k in range(3):
@@ -338,11 +340,10 @@
     take(y_rows, y_count - 1, row_sem.at[1])
     for half in range(2):
         take(sends.at[half], depth_count - 1, send_sem.at[half])
-    for half in range(2):
-        take(boxes.at[half], depth_count - 1, box_sem.at[half])
     low = lax.broadcasted_iota(I32, (8, 128), 0) < 4
     passed, even, odd = [], [], []
     for half in range(2):
+        take(boxes.at[half], depth_count - 1, box_sem.at[half])
         ahead = jnp.ones((8, 128), F32)
         first = jnp.zeros((8, 128), F32)
         second = jnp.zeros((8, 128), F32)

time: 20.3 us -> 20.2 us (level)
  no operation moved by 1% of the time
where the time goes in v8:
time: 20.2 us; the launch traced here: 20.1 us
  Pallas kernels  18.3 us (91%)
  between operations  1.18 us (6%)
  local copies, waits for them, and re-layouts  0.6 us (3%)
    pallas_call x1, Pallas kernels, local(): pl.pallas_call(functools.partial(kernel, depth_count, x_count, y_count),...  18.3 us
    unnamed x1, local copies, waits for them, and re-layouts  0.6 us

profile of v8, /device:TPU:1, one launch (start us, length us, event | category | flops | bytes accessed | tf_op | source)
XLA Modules:
  0.0 20.1 jit_solution(10461460975149595334)
XLA Ops:
  0.6 18.3 %render.1 = (f32[4,8,128]{2,1,0:T(8,128)S(1)}, f32[1,1]{1,0:T(1,128)S(1)}) custom-call(bf16[1,16,32,1024]{3,2,1,0:T(8,128)(2,1)} %bricks.1, s32[1,16]{1,0:T(1,128)} %levels_in.1, s32[1,16,1024]{2,1,0:T(8,128)} %counts.1, f32[1,16]{1,0:T(1,128)} %gains_in.1, s32[1,16,32]{2,1,0:T(8,128)} %bitcast.3, f32[3]{0:T(128)} %slope_in.1), custom_call_target="tpu_custom_call" | custom-call | tf_op jit(solution)/shard_map/render/pallas_call | solution.py:377
  19.4 0.6 %copy.11 = f32[4,1,1024]{2,1,0:T(1,128)} copy(f32[4,1,1024]{2,1,0:T(1,128)S(1)} %bitcast.2) | data formatting | bytes 32768

commit v9 on v8

--- a/solution.py
+++ b/solution.py
@@ -120,7 +120,7 @@
         for i in range(4)
     ]
     fetch_lives = [
-        pltpu.make_async_copy(counts.at[0, :, pl.ds(j * 128, 128)], lives.at[j], live_sem.at[j])
+        pltpu.make_async_copy(counts.at[0, :, pl.ds(j * 128, 128)], lives.at[j, pl.ds(0, 16)], live_sem.at[j])
         for j in range(8)
     ]
     for copy in fetch_bricks + fetch_small + fetch_lives:
@@ -388,7 +388,7 @@
             pltpu.SMEM((3,), F32),
             pltpu.VMEM((16, tile_count), I32),
             pltpu.VMEM((16, 32, 1024), BF16),
-            pltpu.VMEM((8, 16, 128), I32),
+            pltpu.VMEM((8, 24, 128), I32),
             pltpu.VMEM((256, 768), BF16),
             pltpu.VMEM((768, 1024), BF16),
             pltpu.VMEM((512, 1024), BF16),

time: 20.2 us -> 20.2 us (level)
  no operation moved by 1% of the time
where the time goes in v9:
time: 20.2 us; the launch traced here: 20 us
  Pallas kernels  18.3 us (91%)
  between operations  1.18 us (6%)
  local copies, waits for them, and re-layouts  0.6 us (3%)
    pallas_call x1, Pallas kernels, local(): pl.pallas_call(functools.partial(kernel, depth_count, x_count, y_count),...  18.3 us
    unnamed x1, local copies, waits for them, and re-layouts  0.6 us

profile of v9, /device:TPU:1, one launch (start us, length us, event | category | flops | bytes accessed | tf_op | source)
XLA Modules:
  0.0 20.0 jit_solution(2279284052528293720)
XLA Ops:
  0.6 18.3 %render.1 = (f32[4,8,128]{2,1,0:T(8,128)S(1)}, f32[1,1]{1,0:T(1,128)S(1)}) custom-call(bf16[1,16,32,1024]{3,2,1,0:T(8,128)(2,1)} %bricks.1, s32[1,16]{1,0:T(1,128)} %levels_in.1, s32[1,16,1024]{2,1,0:T(8,128)} %counts.1, f32[1,16]{1,0:T(1,128)} %gains_in.1, s32[1,16,32]{2,1,0:T(8,128)} %bitcast.3, f32[3]{0:T(128)} %slope_in.1), custom_call_target="tpu_custom_call" | custom-call | tf_op jit(solution)/shard_map/render/pallas_call | solution.py:377
  19.4 0.6 %copy.11 = f32[4,1,1024]{2,1,0:T(1,128)} copy(f32[4,1,1024]{2,1,0:T(1,128)S(1)} %bitcast.2) | data formatting | bytes 32768
